TPU v7x, 512 devices: a whole 4x8x8 slice. The times are simulated.
512 devices in a mesh: tm: 8 (over z_lo, x), tile: 64 (over y, z_hi, core).
Axes of the slice: x: 4, y: 8, z: 8 (z_hi: 4, z_lo: 2; z = z_hi * 2 + z_lo), core: 2. Of those that a mesh axis runs over, the one named last changes fastest.
Arguments:
- inputs: bfloat16 [16, 64, 24576], P('tm', 'tile'), may hold values from -80 to 80
- cotangent: bfloat16 [16, 64, 24576], P('tm', 'tile'), may hold values from -6 to 6
- frame_weight: int32 [16], P('tm'), may hold values from 1 to 4
- gain_one: float32 [192], replicated, may hold values from 0.1 to 1.9
- conv_one: bfloat16 [3, 3, 3, 192, 192], replicated, may hold values from -0.078125 to 0.078125
- gain_two: float32 [192], replicated, may hold values from 0.1 to 1.9
- conv_two: bfloat16 [3, 3, 3, 192, 192], replicated, may hold values from -0.078125 to 0.078125
Outputs:
- input_grad: bfloat16 [16, 64, 24576], P('tm', None, 'tile')
All inputs are finite; a program needn't handle non-finite values.
Results may differ from a plain program's by a relative error of at most 0.0059.
Values may be sent and summed in bfloat16 or wider, within the bound.
No kernel may reach another device: no remote copies, remote signals or barrier semaphores. Data moves between devices by JAX's collectives and lax.ppermute only.
A program may use at most 128 MiB of HBM per device.

v0:
```python
import jax
import jax.numpy as jnp
from jax import lax
from jax.experimental import pallas as pl
from jax.experimental.pallas import tpu as pltpu
from jax.sharding import Mesh
from jax.sharding import PartitionSpec as P

EPS = 1e-06
F32, BF16 = jnp.float32, jnp.bfloat16
MIB = 1024 * 1024


def shifted(value, axis, steps):
    count = lax.axis_size(axis)
    first, last = (max(0, -steps), min(count, count - steps))
    return lax.ppermute(value, axis, [(source, source + steps) for source in range(first, last)])


def spread(value):
    count = lax.axis_size("tm")
    later = [(2 * k, 2 * k + 2) for k in range(count - 1)]
    earlier = [(2 * k + 3, 2 * k + 1) for k in range(count - 1)]
    return lax.ppermute(value, ("tm", "core"), later + earlier)


def pack_kernel(weight, x, c, out, scale, x_here, dy, sems):
    tiles, frames, wide = out.shape
    pair = wide // 4
    moves = [
        pltpu.make_async_copy(src, dst, sems.at[n])
        for n, (src, dst) in enumerate(((weight, scale), (c, dy), (x, x_here)))
    ]
    for move in moves:
        move.start()
    none = jnp.zeros((frames, pair), BF16)
    for core in range(2):
        out[core, :, :pair] = none
        out[tiles - 2 + core, :, 3 * pair :] = none
    for move in moves[:2]:
        move.wait()
    at = lax.broadcasted_iota(jnp.int32, dy.shape, 0)
    factor = jnp.where(at == 0, scale[0].astype(F32), scale[1].astype(F32))
    dy[...] = (dy[...].astype(F32) * factor).astype(BF16)
    moves[2].wait()
    for q in range(tiles // 2):
        first, last = max(0, 2 * q - 1), min(tiles, 2 * q + 3)
        skip = first - (2 * q - 1)
        for core, src in ((0, x_here), (1, dy)):
            out[2 * q + core, :, skip * pair : (skip + last - first) * pair] = src[:, first * pair : last * pair]


def turn_kernel(conv_one, conv_two, one, two):
    width = conv_one.shape[-1]
    for src, dst in ((conv_two, two), (conv_one, one)):
        for a in range(3):
            for b in range(3):
                for e in range(3):
                    dst[a, b, :, e * width : (e + 1) * width] = src[2 - a, 2 - b, 2 - e]


def lefts(field, columns, width):
    odd = field[:, width:]
    parts = []
    for c in range(columns):
        src, at = (field, c) if c % 2 == 0 else (odd, c - 1)
        parts.append(src[:, at * width : (at + 3) * width])
    return jnp.concatenate(parts, axis=0)


def conv_sum(terms, kern, flipped, rows):
    dims = (((1,), (1 if flipped else 0,)), ((), ()))
    taps = []
    for b in range(3):
        total = None
        for a, left in terms:
            right = kern[a, b]
            if not flipped:
                right = right.reshape(left.shape[1], right.shape[-1])
            part = lax.dot_general(left, right, dims, preferred_element_type=F32)
            total = part if total is None else total + part
        taps.append(total)
    group = rows // 8
    at = lax.broadcasted_iota(jnp.int32, (group, taps[0].shape[1]), 0)
    blocks = []
    for first in range(0, taps[0].shape[0], rows):
        above, here, below = (tap[first : first + rows] for tap in taps)
        wrap = jnp.where(at == 0, 0.0, pltpu.roll(above[rows - group :], 1, 0))
        above = jnp.concatenate([wrap, above[: rows - group]], axis=0)
        wrap = jnp.where(at == group - 1, 0.0, pltpu.roll(below[:group], group - 1, 0))
        below = jnp.concatenate([below[group:], wrap], axis=0)
        blocks.append(here + above + below)
    return blocks


def scale_of(value):
    return lax.rsqrt(jnp.sum(value * value, axis=-1, keepdims=True) * (1.0 / value.shape[-1]) + EPS)


def sigmoid(value):
    return 0.5 * jnp.tanh(0.5 * value) + 0.5


def norm_back(value, gain, grad):
    scale = scale_of(value)
    normed = value * scale
    act = normed * gain
    sig = sigmoid(act)
    d_norm = grad * sig * (1.0 + act * (1.0 - sig)) * gain
    mean = jnp.sum(d_norm * normed, axis=-1, keepdims=True) * (1.0 / value.shape[-1])
    return scale * (d_norm - normed * mean)


def hidden(core, src, gain, hid):
    width = gain.shape[-1]
    rows = src.shape[2]
    first = lax.broadcasted_iota(jnp.int32, (rows, 2 * width), 1) < width
    gains = jnp.concatenate([gain, gain], axis=1)
    for frame in range(2):
        for p in range(3):
            lanes = pl.ds(pl.multiple_of((p + core) * 2 * width, 2 * width), 2 * width)
            value = src[0, frame, :, lanes].astype(F32)
            square = value * value
            left = jnp.sum(jnp.where(first, square, 0.0), axis=-1, keepdims=True)
            right = jnp.sum(jnp.where(first, 0.0, square), axis=-1, keepdims=True)
            left, right = (lax.rsqrt(part * (1.0 / width) + EPS) for part in (left, right))
            act = value * jnp.where(first, left, right) * gains
            hid[frame, :, p * 2 * width : (p + 1) * 2 * width] = (act * sigmoid(act)).astype(BF16)


def fields_of(core, src, gain, hid):
    width = gain.shape[-1]
    hidden(core, src, gain, hid)
    lanes = pl.ds(pl.multiple_of(core * 2 * width, 2 * width), 6 * width)
    return [lefts(hid[f], 4, width) for f in range(2)], [lefts(src[1, f, :, lanes], 4, width) for f in range(2)]


def own_kernel(place, own, gain_one, conv_one, turned, z_part, d_part, hid):
    rows = own.shape[2]
    xs, gs = fields_of(place[0], own, gain_one[...], hid)
    for t, terms in enumerate(([(2, xs[0])], [(1, xs[0]), (2, xs[1])])):
        for c, block in enumerate(conv_sum(terms, conv_one, False, rows)):
            z_part[t, c] = block
    for t, terms in enumerate(([(0, gs[0]), (1, gs[1])], [(0, gs[1])])):
        for c, block in enumerate(conv_sum(terms, turned, True, rows)):
            d_part[t, c] = block


def middle_kernel(
    place, other, z_part, d_part, two, gain_one, gain_two, conv_one, one, out, send, hid, z_all, d_all
):
    width = gain_one.shape[-1]
    rows = other.shape[2]
    xs, gs = fields_of(place[0], other, gain_one[...], hid)
    for t, terms in enumerate(([(0, xs[0]), (1, xs[1])], [(0, xs[1])])):
        for c, block in enumerate(conv_sum(terms, conv_one, False, rows)):
            z_all[t, c] = z_part[t, c] + block
    for t, terms in enumerate(([(2, gs[0])], [(1, gs[0]), (2, gs[1])])):
        for c, block in enumerate(conv_sum(terms, two, True, rows)):
            d_all[t, c] = d_part[t, c] + block
    for t in range(2):
        for c in range(4):
            d_z = norm_back(z_all[t, c], gain_two[...], d_all[t, c])
            if c in (0, 3):
                d_z = jnp.where(place[1 + c // 3] == 0, 0.0, d_z)
            out[t, :, c * width : (c + 1) * width] = d_z.astype(BF16)
    ds = [lefts(out[f], 2, width) for f in range(2)]
    for t, terms in enumerate(([(2, ds[0])], [(1, ds[0]), (2, ds[1])])):
        for c, block in enumerate(conv_sum(terms, one, True, rows)):
            send[t, :, c * width : (c + 1) * width] = block.astype(BF16)


def halves(first, value):
    left = jnp.sum(jnp.where(first, value, 0.0), axis=-1, keepdims=True)
    right = jnp.sum(jnp.where(first, 0.0, value), axis=-1, keepdims=True)
    return jnp.where(first, left, right)


def early_kernel(place, own, d_own, one, gain_one, base, slope, along, across, d_all):
    width = gain_one.shape[-1]
    rows = own.shape[2]
    ds = [lefts(d_own[f], 2, width) for f in range(2)]
    for t, terms in enumerate(([(0, ds[0]), (1, ds[1])], [(0, ds[1])])):
        for c, block in enumerate(conv_sum(terms, one, True, rows)):
            d_all[t, :, c * width : (c + 1) * width] = block
    lanes = pl.ds(pl.multiple_of((1 + place[0]) * 2 * width, 2 * width), 2 * width)
    first = lax.broadcasted_iota(jnp.int32, (rows, 2 * width), 1) < width
    gain = jnp.concatenate([gain_one[...]] * 2, axis=1)
    for t in range(2):
        value = own[0, t, :, lanes].astype(F32)
        scale = lax.rsqrt(halves(first, value * value) * (1.0 / width) + EPS)
        normed = value * scale
        act = normed * gain
        sig = sigmoid(act)
        turn = sig * (1.0 + act * (1.0 - sig)) * gain
        slope[t] = scale * turn
        along[t] = scale * normed * (1.0 / width)
        across[t] = turn * normed
        grad = d_all[t]
        total = halves(first, across[t] * grad)
        base[t] = own[1, t, :, lanes].astype(F32) + slope[t] * grad - along[t] * total


def last_kernel(late, base, slope, along, across, out, natural):
    rows = out.shape[1]
    group = rows // 8
    first = lax.broadcasted_iota(jnp.int32, late.shape[1:], 1) < late.shape[2] // 2
    for t in range(2):
        grad = late[t].astype(F32)
        result = base[t] + slope[t] * grad - along[t] * halves(first, across[t] * grad)
        for p in range(natural.shape[0]):
            for r in range(8):
                piece = result[r * group : (r + 1) * group, p * 128 : (p + 1) * 128]
                natural[p, pl.ds(r, group, stride=8), :] = piece
        for p in range(natural.shape[0]):
            out[t, :, p * 128 : (p + 1) * 128] = natural[p].astype(BF16)


def call(kernel, ins, outs, scratch, flops, *args, limit=16 * MIB):
    kinds = {"v": pltpu.VMEM, "s": pltpu.SMEM, "h": pltpu.HBM}
    return pl.pallas_call(
        kernel,
        out_shape=outs,
        in_specs=[pl.BlockSpec(memory_space=kinds[kind]) for kind in ins],
        out_specs=jax.tree.map(lambda _: pl.BlockSpec(memory_space=pltpu.VMEM), outs),
        scratch_shapes=scratch,
        compiler_params=pltpu.CompilerParams(vmem_limit_bytes=limit),
        cost_estimate=pl.CostEstimate(flops=flops, bytes_accessed=4 << 20, transcendentals=0),
    )(*args)


def body(inputs, cotangent, frame_weight, gain_one, conv_one, gain_two, conv_two):
    core = lax.axis_index("core")
    tiles, me = lax.axis_size(("chip", "core")), lax.axis_index(("chip", "core"))
    frames, _, merged = inputs.shape
    width = gain_one.shape[0]
    wide = 8 * width
    gain_one, gain_two = gain_one.reshape(1, width), gain_two.reshape(1, width)
    place = jnp.stack([core, me > 0, me < tiles - 1]).astype(jnp.int32)
    array = jax.ShapeDtypeStruct
    one = 2 * tiles * 9 * width * width

    local = [pltpu.SMEM((frames,), jnp.int32)] + [pltpu.VMEM((frames, merged), BF16)] * 2
    blocks = call(
        pack_kernel, "hhh", array((tiles, frames, wide), BF16), local + [pltpu.SemaphoreType.DMA((3,))], 10**6,
        frame_weight, inputs.reshape(frames, merged), cotangent.reshape(frames, merged), limit=60 * MIB,
    )
    held = lax.all_to_all(blocks, ("chip", "core"), 0, 0)
    held = held.reshape(tiles // 8, 8, frames, wide).transpose(2, 1, 0, 3).reshape(frames, tiles, wide)
    turned = array((3, 3, width, 3 * width), BF16)
    turned_one, turned_two = call(turn_kernel, "vv", (turned, turned), [], 10**9, conv_one, conv_two)
    held, turned_one, turned_two = lax.optimization_barrier((held, turned_one, turned_two))
    arrived = spread(held)
    own = lax.all_gather(held, "core")
    sums = (frames, 4, tiles, width)
    hid = pltpu.VMEM((frames, tiles, 6 * width), BF16)
    z_part, d_part = call(
        own_kernel, "svvvv", (array(sums, F32), array(sums, F32)), [hid], 24 * one,
        place, own, gain_one, conv_one, turned_two,
    )
    other = lax.all_gather(arrived, "core")
    d_own, send = call(
        middle_kernel, "svvvvvvvv",
        (array((frames, tiles, 4 * width), BF16), array((frames, tiles, 2 * width), BF16)),
        [hid, pltpu.VMEM(sums, F32), pltpu.VMEM(sums, F32)], 24 * one,
        place, other, z_part, d_part, turned_two, gain_one, gain_two, conv_one, turned_one,
    )
    late = shifted(send, "tm", -1)
    field = (frames, tiles, 2 * width)
    parts = call(
        early_kernel, "svvvv", (array(field, F32),) * 4, [pltpu.VMEM(field, F32)], 6 * one,
        place, own, d_own, turned_one, gain_one,
    )
    natural = pltpu.VMEM((2 * width // 128, tiles, 128), F32)
    return call(last_kernel, "vvvvv", array(field, BF16), [natural], one, late, *parts)


def solution(mesh):
    tm, tile = mesh.devices.shape
    chips = Mesh(mesh.devices.reshape(tm, tile // 2, 2), ("tm", "chip", "core"))
    tiles = ("chip", "core")
    in_specs = (P("tm", tiles, None), P("tm", tiles, None), P("tm"), P(), P(), P(), P())
    out_specs = P("tm", None, tiles)
    return jax.shard_map(body, mesh=chips, in_specs=in_specs, out_specs=out_specs, check_vma=False)
```

profile of v0, /device:TPU:6, one launch (start us, length us, event | category | flops | bytes accessed | tf_op | source)
XLA Modules:
  0.0 62.8 jit_solution(17530874126469572311)
XLA Ops:
  0.0 1.8 %shard_map.73 = bf16[64,2,1536]{2,1,0:T(2,128)(2,1)} custom-call(s32[2]{0:T(128)} %weight.1, bf16[2,24576]{1,0:T(2,128)(2,1)} %bitcast.25, bf16[2,24576]{1,0:T(2,128)(2,1)} %bitcast.26), custom_call_target="tpu_custom_call" | custom-call | flops 1000000 | bytes 4194304 | tf_op jit(solution)/shard_map/pallas_call | solution.py:221
  1.8 16.6 %all-to-all-start = ((bf16[64,2,1536]{2,1,0:T(2,128)(2,1)}), bf16[64,2,1536]{2,1,0:T(2,128)(2,1)S(1)}, u32[]{:S(2)}, u32[]{:S(2)}) async-start(bf16[64,2,1536]{2,1,0:T(2,128)(2,1)} %shard_map.73), calls=%async_computation | async-start | bytes 786432 | tf_op jit(solution)/shard_map/all_to_all | solution.py:248
  18.4 0.0 copy-start
  18.4 1.7 %copy-done = bf16[3,3,3,192,192]{4,3,2,1,0:T(8,128)(2,1)S(1)} copy-done((bf16[3,3,3,192,192]{4,3,2,1,0:T(8,128)(2,1)S(1)}, bf16[3,3,3,192,192]{4,3,2,1,0:T(8,128)(2,1)}, u32[]{:S(2)}) %copy-start) | copy-done | bytes 1990680
  20.2 0.0 copy-start.6
  20.2 1.7 %copy-done.6 = bf16[3,3,3,192,192]{4,3,2,1,0:T(8,128)(2,1)S(1)} copy-done((bf16[3,3,3,192,192]{4,3,2,1,0:T(8,128)(2,1)S(1)}, bf16[3,3,3,192,192]{4,3,2,1,0:T(8,128)(2,1)}, u32[]{:S(2)}) %copy-start.6) | copy-done | bytes 1990680
  21.9 0.0 copy-start.1
  21.9 0.0 copy-start.7
  21.9 0.6 shard_map.74
  22.5 0.0 copy-start.2
  22.5 1.4 %copy-done.2 = bf16[3,3,192,576]{3,2,1,0:T(8,128)(2,1)} copy-done((bf16[3,3,192,576]{3,2,1,0:T(8,128)(2,1)}, bf16[3,3,192,576]{3,2,1,0:T(8,128)(2,1)S(1)}, u32[]{:S(2)}) %copy-start.2) | copy-done | bytes 1990680
  23.9 0.0 copy-start.4
  23.9 1.3 %copy-done.4 = bf16[3,3,192,576]{3,2,1,0:T(8,128)(2,1)} copy-done((bf16[3,3,192,576]{3,2,1,0:T(8,128)(2,1)}, bf16[3,3,192,576]{3,2,1,0:T(8,128)(2,1)S(1)}, u32[]{:S(2)}) %copy-start.4) | copy-done | bytes 1990680
  25.2 10.4 %all-to-all-done = bf16[64,2,1536]{2,1,0:T(2,128)(2,1)S(1)} async-done(((bf16[64,2,1536]{2,1,0:T(2,128)(2,1)}), bf16[64,2,1536]{2,1,0:T(2,128)(2,1)S(1)}, u32[]{:S(2)}, u32[]{:S(2)}) %all-to-all-start) | async-done | bytes 393248 | tf_op jit(solution)/shard_map/all_to_all | solution.py:248
  35.6 0.2 copy.11
  35.9 3.3 %collective-permute-start = (bf16[2,64,1536]{2,1,0:T(8,128)(2,1)S(1)}, bf16[2,64,1536]{2,1,0:T(8,128)(2,1)S(1)}, u32[]{:S(2)}, u32[]{:S(2)}) collective-permute-start(bf16[2,64,1536]{2,1,0:T(8,128)(2,1)S(1)} %bitcast.23), channel_id=1, source_target_pairs={{0,64},{64,128},{128,192},{192,256},{256,320},{320,384},{384,448},... | collective-permute-start | bytes 1179656 | tf_op jit(solution)/shard_map/ppermute | solution.py:24
  39.2 0.1 pad_add_fusion.place
  39.2 2.4 %all-gather.1 = bf16[4,64,1536]{2,1,0:T(8,128)(2,1)S(1)} all-gather(bf16[2,64,1536]{2,1,0:T(8,128)(2,1)S(1)} %bitcast.24), channel_id=3, replica_groups=mesh['tm'=8,'chip'=32,'core'=2] {'core'}, dimensions={0}, use_global_device_ids=true | all-gather | bytes 1179648 | tf_op jit(solution)/shard_map/all_gather | solution.py:254
  41.6 0.0 copy-done.1
  41.6 0.0 copy-done.7
  41.6 0.0 copy-start.3
  41.6 1.6 %copy-done.3 = bf16[3,3,192,576]{3,2,1,0:T(8,128)(2,1)S(1)} copy-done((bf16[3,3,192,576]{3,2,1,0:T(8,128)(2,1)S(1)}, bf16[3,3,192,576]{3,2,1,0:T(8,128)(2,1)}, u32[]{:S(2)}) %copy-start.3) | copy-done | bytes 1990680
  43.2 0.0 copy-start.5
  43.2 0.0 copy-start.8
  43.2 2.9 %shard_map.75 = (f32[2,4,64,192]{3,2,1,0:T(8,128)S(1)}, f32[2,4,64,192]{3,2,1,0:T(8,128)S(1)}) custom-call(s32[3]{0:T(128)S(1)} %pad_add_fusion.place, bf16[2,2,64,1536]{3,2,1,0:T(8,128)(2,1)S(1)} %bitcast.15, f32[1,192]{1,0:T(1,128)S(1)} %bitcast.18, bf16[3,3,3,192,192]{4,3,2,1,0:T(8,128)(2,1)S(1)} %copy-done.1, bf16[3,3,192,576]{3,2,1,0:T(8,128)(2,1)S(1)} %copy-done.3), custom_call_target="tpu_custom_call" | custom-call | flops 1019215872 | bytes 4194304 | tf_op jit(solution)/shard_map/pallas_call | solution.py:221
  46.1 0.0 collective-permute-done
  46.1 2.7 %all-gather = bf16[4,64,1536]{2,1,0:T(8,128)(2,1)S(1)} all-gather(bf16[2,64,1536]{2,1,0:T(8,128)(2,1)S(1)} %collective-permute-done), channel_id=2, replica_groups=mesh['tm'=8,'chip'=32,'core'=2] {'core'}, dimensions={0}, use_global_device_ids=true | all-gather | bytes 1179648 | tf_op jit(solution)/shard_map/all_gather | solution.py:261
  48.8 0.0 copy-done.5
  48.8 0.0 copy-done.8
  48.8 4.2 %shard_map.76 = (bf16[2,64,768]{2,1,0:T(8,128)(2,1)S(1)}, bf16[2,64,384]{2,1,0:T(8,128)(2,1)S(1)}) custom-call(s32[3]{0:T(128)S(1)} %pad_add_fusion.place, bf16[2,2,64,1536]{3,2,1,0:T(8,128)(2,1)S(1)} %bitcast.17, f32[2,4,64,192]{3,2,1,0:T(8,128)S(1)} %get-tuple-element.22.z_part, f32[2,4,64,192]{3,2,1,0:T(8,128)S(1)} %get-tuple-element.23.d_part, ...), custom_call_target="tpu_custom_call" | custom-call | flops 1019215872 | bytes 4194304 | tf_op jit(solution)/shard_map/pallas_call | solution.py:221
  53.0 2.3 %collective-permute-start.1 = (bf16[2,64,384]{2,1,0:T(8,128)(2,1)S(1)}, bf16[2,64,384]{2,1,0:T(8,128)(2,1)S(1)}, u32[]{:S(2)}, u32[]{:S(2)}) collective-permute-start(bf16[2,64,384]{2,1,0:T(8,128)(2,1)S(1)} %get-tuple-element.25), channel_id=1, source_target_pairs={{64,0},{128,64},{192,128},{256,192},{320,256},{384,320},{448,384},... | collective-permute-start | bytes 294920 | tf_op jit(solution)/shard_map/ppermute | solution.py:17
  55.2 1.8 %shard_map.77 = (f32[2,64,384]{2,1,0:T(8,128)S(1)}, f32[2,64,384]{2,1,0:T(8,128)S(1)}, f32[2,64,384]{2,1,0:T(8,128)S(1)}, f32[2,64,384]{2,1,0:T(8,128)S(1)}) custom-call(s32[3]{0:T(128)S(1)} %pad_add_fusion.place, bf16[2,2,64,1536]{3,2,1,0:T(8,128)(2,1)S(1)} %bitcast.16, bf16[2,64,768]{2,1,0:T(8,128)(2,1)S(1)} %get-tuple-element.26.d_own, ...), custom_call_target="tpu_custom_call" | custom-call | flops 254803968 | bytes 4194304 | tf_op jit(solution)/shard_map/pallas_call | solution.py:221
  57.0 5.1 %collective-permute-done.1.late = bf16[2,64,384]{2,1,0:T(8,128)(2,1)S(1)} collective-permute-done((bf16[2,64,384]{2,1,0:T(8,128)(2,1)S(1)}, bf16[2,64,384]{2,1,0:T(8,128)(2,1)S(1)}, u32[]{:S(2)}, u32[]{:S(2)}) %collective-permute-start.1) | collective-permute-done | bytes 98336 | tf_op jit(solution)/shard_map/ppermute | solution.py:17
  62.1 0.8 %shard_map.78 = bf16[2,64,384]{2,1,0:T(8,128)(2,1)} custom-call(bf16[2,64,384]{2,1,0:T(8,128)(2,1)S(1)} %collective-permute-done.1.late, f32[2,64,384]{2,1,0:T(8,128)S(1)} %get-tuple-element.27.base, f32[2,64,384]{2,1,0:T(8,128)S(1)} %get-tuple-element.28.slope, f32[2,64,384]{2,1,0:T(8,128)S(1)} %get-tuple-element.29.along, ...), custom_call_target="tpu_custom_call" | custom-call | flops 42467328 | bytes 4194304 | tf_op jit(solution)/shard_map/pallas_call | solution.py:221
Async XLA Ops:
  1.8 33.8 %all-to-all-start = ((bf16[64,2,1536]{2,1,0:T(2,128)(2,1)}), bf16[64,2,1536]{2,1,0:T(2,128)(2,1)S(1)}, u32[]{:S(2)}, u32[]{:S(2)}) async-start(bf16[64,2,1536]{2,1,0:T(2,128)(2,1)} %shard_map.73), calls=%async_computation | async-start | bytes 786432 | tf_op jit(solution)/shard_map/all_to_all | solution.py:248
  18.4 1.8 %copy-start = (bf16[3,3,3,192,192]{4,3,2,1,0:T(8,128)(2,1)S(1)}, bf16[3,3,3,192,192]{4,3,2,1,0:T(8,128)(2,1)}, u32[]{:S(2)}) copy-start(bf16[3,3,3,192,192]{4,3,2,1,0:T(8,128)(2,1)} %conv_one.5) | copy-start | bytes 5971972
  20.2 1.7 %copy-start.6 = (bf16[3,3,3,192,192]{4,3,2,1,0:T(8,128)(2,1)S(1)}, bf16[3,3,3,192,192]{4,3,2,1,0:T(8,128)(2,1)}, u32[]{:S(2)}) copy-start(bf16[3,3,3,192,192]{4,3,2,1,0:T(8,128)(2,1)} %conv_two.1) | copy-start | bytes 5971972
  21.9 19.7 %copy-start.1 = (bf16[3,3,3,192,192]{4,3,2,1,0:T(8,128)(2,1)S(1)}, bf16[3,3,3,192,192]{4,3,2,1,0:T(8,128)(2,1)}, u32[]{:S(2)}) copy-start(bf16[3,3,3,192,192]{4,3,2,1,0:T(8,128)(2,1)} %conv_one.5) | copy-start | bytes 5971972
  21.9 19.7 %copy-start.7 = (f32[192]{0:T(256)S(1)}, f32[192]{0:T(256)}, u32[]{:S(2)}) copy-start(f32[192]{0:T(256)} %param.10) | copy-start | bytes 2308
  22.5 1.4 %copy-start.2 = (bf16[3,3,192,576]{3,2,1,0:T(8,128)(2,1)}, bf16[3,3,192,576]{3,2,1,0:T(8,128)(2,1)S(1)}, u32[]{:S(2)}) copy-start(bf16[3,3,192,576]{3,2,1,0:T(8,128)(2,1)S(1)} %get-tuple-element.21.turned.two) | copy-start | bytes 5971972
  23.9 1.3 %copy-start.4 = (bf16[3,3,192,576]{3,2,1,0:T(8,128)(2,1)}, bf16[3,3,192,576]{3,2,1,0:T(8,128)(2,1)S(1)}, u32[]{:S(2)}) copy-start(bf16[3,3,192,576]{3,2,1,0:T(8,128)(2,1)S(1)} %get-tuple-element.24.one) | copy-start | bytes 5971972
  35.9 10.2 %collective-permute-start = (bf16[2,64,1536]{2,1,0:T(8,128)(2,1)S(1)}, bf16[2,64,1536]{2,1,0:T(8,128)(2,1)S(1)}, u32[]{:S(2)}, u32[]{:S(2)}) collective-permute-start(bf16[2,64,1536]{2,1,0:T(8,128)(2,1)S(1)} %bitcast.23), channel_id=1, source_target_pairs={{0,64},{64,128},{128,192},{192,256},{256,320},{320,384},{384,448},... | collective-permute-start | bytes 1179656 | tf_op jit(solution)/shard_map/ppermute | solution.py:24
  41.6 1.6 %copy-start.3 = (bf16[3,3,192,576]{3,2,1,0:T(8,128)(2,1)S(1)}, bf16[3,3,192,576]{3,2,1,0:T(8,128)(2,1)}, u32[]{:S(2)}) copy-start(bf16[3,3,192,576]{3,2,1,0:T(8,128)(2,1)} %copy-done.2) | copy-start | bytes 5971972
  43.2 5.5 %copy-start.5 = (bf16[3,3,192,576]{3,2,1,0:T(8,128)(2,1)S(1)}, bf16[3,3,192,576]{3,2,1,0:T(8,128)(2,1)}, u32[]{:S(2)}) copy-start(bf16[3,3,192,576]{3,2,1,0:T(8,128)(2,1)} %copy-done.4) | copy-start | bytes 5971972
  43.2 5.5 %copy-start.8 = (f32[192]{0:T(256)S(1)}, f32[192]{0:T(256)}, u32[]{:S(2)}) copy-start(f32[192]{0:T(256)} %param.12) | copy-start | bytes 2308
  53.0 9.1 %collective-permute-start.1 = (bf16[2,64,384]{2,1,0:T(8,128)(2,1)S(1)}, bf16[2,64,384]{2,1,0:T(8,128)(2,1)S(1)}, u32[]{:S(2)}, u32[]{:S(2)}) collective-permute-start(bf16[2,64,384]{2,1,0:T(8,128)(2,1)S(1)} %get-tuple-element.25), channel_id=1, source_target_pairs={{64,0},{128,64},{192,128},{256,192},{320,256},{384,320},{448,384},... | collective-permute-start | bytes 294920 | tf_op jit(solution)/shard_map/ppermute | solution.py:17
where the time goes:
time: 63.2 us; the launch traced here: 62.8 us
  starting transfers between devices  22.1 us (35%)
  waiting for transfers between devices  15.5 us (25%)
  Pallas kernels  12 us (19%)
  local copies, waits for them, and re-layouts  8.04 us (13%)
  blocking collectives  5.02 us (8%)
    all_to_all x1, starting transfers between devices, body(): held = lax.all_to_all(blocks, ('chip', 'core'), 0, 0)  16.6 us
    pallas_call x6, Pallas kernels, call(): pl.pallas_call(kernel, out_shape=outs, in_specs=[pl.BlockSpec(memory_spac...  12 us
    all_to_all x1, waiting for transfers between devices, body(): held = lax.all_to_all(blocks, ('chip', 'core'), 0, 0)  10.4 us
    unnamed x18, local copies, waits for them, and re-layouts  7.82 us
    ppermute x1, waiting for transfers between devices, shifted(): lax.ppermute(value, axis, [(source, source + steps) for source in range(f...  5.05 us
    ppermute x1, starting transfers between devices, spread(): return lax.ppermute(value, ('tm', 'core'), later + earlier)  3.3 us
    all_gather x1, blocking collectives, body(): other = lax.all_gather(arrived, 'core')  2.66 us
    all_gather x1, blocking collectives, body(): own = lax.all_gather(held, 'core')  2.36 us
  transfers between devices with their start and end apart: 3, of which 2 were waited for; matrix products, arithmetic and copies ran while one was open for 0% of the time, Pallas kernels for 8%

commit v1 on v0

v1 whole, which is shorter than its diff:
```python
import jax
import jax.numpy as jnp
from jax import lax
from jax.experimental import pallas as pl
from jax.experimental.pallas import tpu as pltpu
from jax.sharding import Mesh
from jax.sharding import PartitionSpec as P

EPS = 1e-06
F32, BF16 = jnp.float32, jnp.bfloat16
MIB = 1024 * 1024


def shifted(value, axis, steps):
    count = lax.axis_size(axis)
    first, last = (max(0, -steps), min(count, count - steps))
    return lax.ppermute(value, axis, [(source, source + steps) for source in range(first, last)])


def spread(value):
    count = lax.axis_size("tm")
    later = [(2 * k, 2 * k + 2) for k in range(count - 1)]
    earlier = [(2 * k + 3, 2 * k + 1) for k in range(count - 1)]
    return lax.ppermute(value, ("tm", "core"), later + earlier)


def pack_kernel(weight, x, c, out, scale, x_here, dy, x_blocks, dy_blocks, sems):
    chips, _, frames, wide = out.shape
    pair = wide // 4
    moves = [
        pltpu.make_async_copy(src, dst, sems.at[n])
        for n, (src, dst) in enumerate(((x, x_here), (c, dy), (weight, scale)))
    ]
    for move in moves:
        move.start()

    def lay(src, blocks, kind):
        none = jnp.zeros((frames, pair), BF16)
        blocks[0, :, :pair] = none
        blocks[chips - 1, :, 3 * pair :] = none
        for q in range(chips):
            first, last = max(0, 2 * q - 1), min(2 * chips, 2 * q + 3)
            skip = first - (2 * q - 1)
            blocks[q, :, skip * pair : (skip + last - first) * pair] = src[:, first * pair : last * pair]
        move = pltpu.make_async_copy(blocks, out.at[:, kind], sems.at[3 + kind])
        move.start()
        return move

    moves[0].wait()
    x_move = lay(x_here, x_blocks, 0)
    moves[1].wait()
    moves[2].wait()
    at = lax.broadcasted_iota(jnp.int32, dy.shape, 0)
    factor = jnp.where(at == 0, scale[0].astype(F32), scale[1].astype(F32)).astype(BF16)
    dy[...] = dy[...] * factor
    dy_move = lay(dy, dy_blocks, 1)
    x_move.wait()
    dy_move.wait()


def turn_kernel(conv_one, conv_two, one, two):
    width = conv_one.shape[-1]
    for src, dst in ((conv_two, two), (conv_one, one)):
        for a in range(3):
            for b in range(3):
                for e in range(3):
                    dst[a, b, :, e * width : (e + 1) * width] = src[2 - a, 2 - b, 2 - e]


def lefts(field, columns, width):
    odd = field[:, width:]
    parts = []
    for c in range(columns):
        src, at = (field, c) if c % 2 == 0 else (odd, c - 1)
        parts.append(src[:, at * width : (at + 3) * width])
    return jnp.concatenate(parts, axis=0)


def conv_sum(terms, kern, flipped, rows):
    dims = (((1,), (1 if flipped else 0,)), ((), ()))
    taps = []
    for b in range(3):
        total = None
        for a, left in terms:
            right = kern[a, b]
            if not flipped:
                right = right.reshape(left.shape[1], right.shape[-1])
            part = lax.dot_general(left, right, dims, preferred_element_type=F32)
            total = part if total is None else total + part
        taps.append(total)
    group = rows // 8
    at = lax.broadcasted_iota(jnp.int32, (group, taps[0].shape[1]), 0)
    blocks = []
    for first in range(0, taps[0].shape[0], rows):
        above, here, below = (tap[first : first + rows] for tap in taps)
        wrap = jnp.where(at == 0, 0.0, pltpu.roll(above[rows - group :], 1, 0))
        above = jnp.concatenate([wrap, above[: rows - group]], axis=0)
        wrap = jnp.where(at == group - 1, 0.0, pltpu.roll(below[:group], group - 1, 0))
        below = jnp.concatenate([below[group:], wrap], axis=0)
        blocks.append(here + above + below)
    return blocks


def scale_of(value):
    return lax.rsqrt(jnp.sum(value * value, axis=-1, keepdims=True) * (1.0 / value.shape[-1]) + EPS)


def norm_back(value, gain, grad):
    scale = scale_of(value)
    normed = value * scale
    half = 0.5 * gain
    h = normed * half
    t = jnp.tanh(h)
    d_norm = grad * ((1.0 + t) * (1.0 + h - h * t)) * half
    mean = jnp.sum(d_norm * normed, axis=-1, keepdims=True) * (1.0 / value.shape[-1])
    return scale * (d_norm - normed * mean)


def thirds(value):
    part = value.shape[-1] // 3
    return [value[:, p * part : (p + 1) * part] for p in range(3)]


def two_sums(value):
    left, middle, right = thirds(value)
    first = lax.broadcasted_iota(jnp.int32, middle.shape, 1) < middle.shape[1] // 2
    left = jnp.sum(left + jnp.where(first, middle, 0.0), axis=-1, keepdims=True)
    right = jnp.sum(right + jnp.where(first, 0.0, middle), axis=-1, keepdims=True)
    return left, right, first


def hidden(core, src, gain, hid):
    width = gain.shape[-1]
    part = 2 * width // 3
    gains = thirds(jnp.concatenate([gain, gain], axis=1))
    for frame in range(2):
        for p in range(3):
            lanes = pl.ds(pl.multiple_of((p + core) * 2 * width, 2 * width), 2 * width)
            value = src[0, frame, :, lanes].astype(F32)
            left, right, first = two_sums(value * value)
            left, right = (0.5 * lax.rsqrt(total * (1.0 / width) + EPS) for total in (left, right))
            scales = left, jnp.where(first, left, right), right
            for n, (piece, scale, g) in enumerate(zip(thirds(value), scales, gains)):
                h = piece * scale * g
                at = p * 2 * width + n * part
                hid[frame, :, at : at + part] = (h + h * jnp.tanh(h)).astype(BF16)


def fields_of(core, src, gain, hid):
    width = gain.shape[-1]
    hidden(core, src, gain, hid)
    lanes = pl.ds(pl.multiple_of(core * 2 * width, 2 * width), 6 * width)
    return [lefts(hid[f], 4, width) for f in range(2)], [lefts(src[1, f, :, lanes], 4, width) for f in range(2)]


def own_kernel(own, gain_one, conv_one, turned, z_part, d_part, hid):
    rows = own.shape[2]
    xs, gs = fields_of(lax.axis_index("core"), own, gain_one[...], hid)
    for t, terms in enumerate(([(2, xs[0])], [(1, xs[0]), (2, xs[1])])):
        for c, block in enumerate(conv_sum(terms, conv_one, False, rows)):
            z_part[t, c] = block
    for t, terms in enumerate(([(0, gs[0]), (1, gs[1])], [(0, gs[1])])):
        for c, block in enumerate(conv_sum(terms, turned, True, rows)):
            d_part[t, c] = block


def middle_kernel(
    other, z_part, d_part, two, gain_one, gain_two, conv_one, one, out, send, hid, z_all, d_all
):
    width = gain_one.shape[-1]
    rows = other.shape[2]
    xs, gs = fields_of(lax.axis_index("core"), other, gain_one[...], hid)
    for t, terms in enumerate(([(0, xs[0]), (1, xs[1])], [(0, xs[1])])):
        for c, block in enumerate(conv_sum(terms, conv_one, False, rows)):
            z_all[t, c] = z_part[t, c] + block
    for t, terms in enumerate(([(2, gs[0])], [(1, gs[0]), (2, gs[1])])):
        for c, block in enumerate(conv_sum(terms, two, True, rows)):
            d_all[t, c] = d_part[t, c] + block
    me, last = lax.axis_index(("chip", "core")), lax.axis_size(("chip", "core")) - 1
    outside = {0: me == 0, 3: me == last}

    def back(t):
        for c in range(4):
            d_z = norm_back(z_all[t, c], gain_two[...], d_all[t, c])
            if c in outside:
                d_z = jnp.where(outside[c], 0.0, d_z)
            out[t, :, c * width : (c + 1) * width] = d_z.astype(BF16)
        return lefts(out[t], 2, width)

    def give(t, blocks):
        for c, block in enumerate(blocks):
            send[t, :, c * width : (c + 1) * width] = block.astype(BF16)

    d_first = back(0)
    give(0, conv_sum([(2, d_first)], one, True, rows))
    middle = conv_sum([(1, d_first)], one, True, rows)
    late = conv_sum([(2, back(1))], one, True, rows)
    give(1, [a + b for a, b in zip(middle, late)])


def halves(value):
    left, right, first = two_sums(value)
    shape = first.shape
    pieces = jnp.broadcast_to(left, shape), jnp.where(first, left, right), jnp.broadcast_to(right, shape)
    return jnp.concatenate(pieces, axis=1)


def early_kernel(own, d_own, one, gain_one, base, slope, along, across, d_all):
    width = gain_one.shape[-1]
    rows = own.shape[2]
    ds = [lefts(d_own[f], 2, width) for f in range(2)]
    for t, terms in enumerate(([(0, ds[0]), (1, ds[1])], [(0, ds[1])])):
        for c, block in enumerate(conv_sum(terms, one, True, rows)):
            d_all[t, :, c * width : (c + 1) * width] = block
    lanes = pl.ds(pl.multiple_of((1 + lax.axis_index("core")) * 2 * width, 2 * width), 2 * width)
    gain = jnp.concatenate([gain_one[...]] * 2, axis=1)
    for t in range(2):
        value = own[0, t, :, lanes].astype(F32)
        scale = lax.rsqrt(halves(value * value) * (1.0 / width) + EPS)
        normed = value * scale
        h = normed * (0.5 * gain)
        bend = jnp.tanh(h)
        turn = (1.0 + bend) * (1.0 + h - h * bend) * (0.5 * gain)
        slope[t] = scale * turn
        along[t] = scale * normed * (1.0 / width)
        across[t] = turn * normed
        grad = d_all[t]
        total = halves(across[t] * grad)
        base[t] = own[1, t, :, lanes].astype(F32) + slope[t] * grad - along[t] * total


def last_kernel(late, base, slope, along, across, out, natural):
    rows = out.shape[1]
    group = rows // 8
    for t in range(2):
        grad = late[t].astype(F32)
        result = base[t] + slope[t] * grad - along[t] * halves(across[t] * grad)
        for p in range(natural.shape[0]):
            for r in range(8):
                piece = result[r * group : (r + 1) * group, p * 128 : (p + 1) * 128]
                natural[p, pl.ds(r, group, stride=8), :] = piece
        for p in range(natural.shape[0]):
            out[t, :, p * 128 : (p + 1) * 128] = natural[p].astype(BF16)


def call(kernel, ins, outs, scratch, flops, *args, limit=16 * MIB, to="v"):
    kinds = {"v": pltpu.VMEM, "s": pltpu.SMEM, "h": pltpu.HBM}
    return pl.pallas_call(
        kernel,
        out_shape=outs,
        in_specs=[pl.BlockSpec(memory_space=kinds[kind]) for kind in ins],
        out_specs=jax.tree.map(lambda _: pl.BlockSpec(memory_space=kinds[to]), outs),
        scratch_shapes=scratch,
        compiler_params=pltpu.CompilerParams(vmem_limit_bytes=limit),
        cost_estimate=pl.CostEstimate(flops=flops, bytes_accessed=4 << 20, transcendentals=0),
    )(*args)


def body(inputs, cotangent, frame_weight, gain_one, conv_one, gain_two, conv_two):
    tiles = lax.axis_size(("chip", "core"))
    frames, _, merged = inputs.shape
    width = gain_one.shape[0]
    wide = 8 * width
    gain_one, gain_two = gain_one.reshape(1, width), gain_two.reshape(1, width)
    array = jax.ShapeDtypeStruct
    one = 2 * tiles * 9 * width * width

    local = [pltpu.SMEM((frames,), jnp.int32)] + [pltpu.VMEM((frames, merged), BF16)] * 2
    local += [pltpu.VMEM((tiles // 2, frames, wide), BF16)] * 2
    blocks = call(
        pack_kernel, "hhh", array((tiles // 2, 2, frames, wide), BF16), local + [pltpu.SemaphoreType.DMA((5,))], 10**6,
        frame_weight, inputs.reshape(frames, merged), cotangent.reshape(frames, merged), limit=60 * MIB, to="h",
    ).reshape(tiles, frames, wide)
    held = lax.all_to_all(blocks, ("chip", "core"), 0, 0)
    held = held.reshape(tiles // 8, 8, frames, wide).transpose(2, 1, 0, 3).reshape(frames, tiles, wide)
    turned = array((3, 3, width, 3 * width), BF16)
    turned_one, turned_two = call(turn_kernel, "vv", (turned, turned), [], 10**9, conv_one, conv_two)
    held, turned_one, turned_two = lax.optimization_barrier((held, turned_one, turned_two))
    arrived = spread(held)
    own = lax.all_gather(held, "core")
    sums = (frames, 4, tiles, width)
    hid = pltpu.VMEM((frames, tiles, 6 * width), BF16)
    z_part, d_part = call(
        own_kernel, "vvvv", (array(sums, F32), array(sums, F32)), [hid], 24 * one,
        own, gain_one, conv_one, turned_two,
    )
    other = lax.all_gather(arrived, "core")
    d_own, send = call(
        middle_kernel, "vvvvvvvv",
        (array((frames, tiles, 4 * width), BF16), array((frames, tiles, 2 * width), BF16)),
        [hid, pltpu.VMEM(sums, F32), pltpu.VMEM(sums, F32)], 24 * one,
        other, z_part, d_part, turned_two, gain_one, gain_two, conv_one, turned_one,
    )
    late = shifted(send, "tm", -1)
    field = (frames, tiles, 2 * width)
    parts = call(
        early_kernel, "vvvv", (array(field, F32),) * 4, [pltpu.VMEM(field, F32)], 6 * one,
        own, d_own, turned_one, gain_one,
    )
    natural = pltpu.VMEM((2 * width // 128, tiles, 128), F32)
    return call(last_kernel, "vvvvv", array(field, BF16), [natural], one, late, *parts)


def solution(mesh):
    tm, tile = mesh.devices.shape
    chips = Mesh(mesh.devices.reshape(tm, tile // 2, 2), ("tm", "chip", "core"))
    tiles = ("chip", "core")
    in_specs = (P("tm", tiles, None), P("tm", tiles, None), P("tm"), P(), P(), P(), P())
    out_specs = P("tm", None, tiles)
    return jax.shard_map(body, mesh=chips, in_specs=in_specs, out_specs=out_specs, check_vma=False)
```

time: 63.2 us -> 62.4 us (0.987)
  Pallas kernels: 12 us -> 10.1 us
  waiting for transfers between devices: 15.5 us -> 16.4 us
    pallas_call x6, Pallas kernels: 12 us -> 10.1 us  [call(): pl.pallas_call(kernel, out_shape=outs, in_specs=[pl.BlockSpec(memory_spac...]
    ppermute x1, waiting for transfers between devices: 5.05 us -> 5.96 us  [shifted(): lax.ppermute(value, axis, [(source, source + steps) for source in range(f...]
    unnamed x18 -> x20, local copies, waits for them, and re-layouts: 7.82 us -> 7.85 us
  transfers between devices with their start and end apart: 3 -> 3, of which waited for: 2 -> 2; matrix products, arithmetic and copies ran while one was open for 0% -> 0% of each run, Pallas kernels for 8% -> 7%
where the time goes in v1:
time: 62.4 us; the launch traced here: 62 us
  starting transfers between devices  21.8 us (35%)
  waiting for transfers between devices  16.4 us (26%)
  Pallas kernels  10.1 us (16%)
  local copies, waits for them, and re-layouts  8.07 us (13%)
  blocking collectives  5.61 us (9%)
    all_to_all x1, starting transfers between devices, body(): held = lax.all_to_all(blocks, ('chip', 'core'), 0, 0)  16.6 us
    all_to_all x1, waiting for transfers between devices, body(): held = lax.all_to_all(blocks, ('chip', 'core'), 0, 0)  10.4 us
    pallas_call x6, Pallas kernels, call(): pl.pallas_call(kernel, out_shape=outs, in_specs=[pl.BlockSpec(memory_spac...  10.1 us
    unnamed x20, local copies, waits for them, and re-layouts  7.85 us
    ppermute x1, waiting for transfers between devices, shifted(): lax.ppermute(value, axis, [(source, source + steps) for source in range(f...  5.96 us
    ppermute x1, starting transfers between devices, spread(): return lax.ppermute(value, ('tm', 'core'), later + earlier)  3.3 us
    all_gather x1, blocking collectives, body(): other = lax.all_gather(arrived, 'core')  3.25 us
    all_gather x1, blocking collectives, body(): own = lax.all_gather(held, 'core')  2.37 us
  transfers between devices with their start and end apart: 3, of which 2 were waited for; matrix products, arithmetic and copies ran while one was open for 0% of the time, Pallas kernels for 7%

profile of v1, /device:TPU:6, one launch (start us, length us, event | category | flops | bytes accessed | tf_op | source)
XLA Modules:
  0.0 62.0 jit_solution(11416429427147899297)
XLA Ops:
  0.0 1.7 %shard_map.73 = bf16[32,2,2,1536]{3,2,1,0:T(2,128)(2,1)} custom-call(s32[2]{0:T(128)} %weight.1, bf16[2,24576]{1,0:T(2,128)(2,1)} %bitcast.24, bf16[2,24576]{1,0:T(2,128)(2,1)} %bitcast.25), custom_call_target="tpu_custom_call" | custom-call | flops 1000000 | bytes 4194304 | tf_op jit(solution)/shard_map/pallas_call | solution.py:248
  1.7 16.6 %all-to-all-start = ((bf16[64,2,1536]{2,1,0:T(2,128)(2,1)}), bf16[64,2,1536]{2,1,0:T(2,128)(2,1)S(1)}, u32[]{:S(2)}, u32[]{:S(2)}) async-start(bf16[64,2,1536]{2,1,0:T(2,128)(2,1)} %bitcast.23), calls=%async_computation | async-start | bytes 786432 | tf_op jit(solution)/shard_map/all_to_all | solution.py:274
  18.3 0.0 copy-start
  18.3 1.7 %copy-done = bf16[3,3,3,192,192]{4,3,2,1,0:T(8,128)(2,1)S(1)} copy-done((bf16[3,3,3,192,192]{4,3,2,1,0:T(8,128)(2,1)S(1)}, bf16[3,3,3,192,192]{4,3,2,1,0:T(8,128)(2,1)}, u32[]{:S(2)}) %copy-start) | copy-done | bytes 1990680
  20.1 0.0 copy-start.7
  20.1 1.7 %copy-done.7 = bf16[3,3,3,192,192]{4,3,2,1,0:T(8,128)(2,1)S(1)} copy-done((bf16[3,3,3,192,192]{4,3,2,1,0:T(8,128)(2,1)S(1)}, bf16[3,3,3,192,192]{4,3,2,1,0:T(8,128)(2,1)}, u32[]{:S(2)}) %copy-start.7) | copy-done | bytes 1990680
  21.8 0.0 copy-start.1
  21.8 0.0 copy-start.8
  21.8 0.6 shard_map.74
  22.4 0.0 copy-start.2
  22.4 1.3 %copy-done.2 = bf16[3,3,192,576]{3,2,1,0:T(8,128)(2,1)} copy-done((bf16[3,3,192,576]{3,2,1,0:T(8,128)(2,1)}, bf16[3,3,192,576]{3,2,1,0:T(8,128)(2,1)S(1)}, u32[]{:S(2)}) %copy-start.2) | copy-done | bytes 1990680
  23.8 0.0 copy-start.4
  23.8 1.4 %copy-done.4 = bf16[3,3,192,576]{3,2,1,0:T(8,128)(2,1)} copy-done((bf16[3,3,192,576]{3,2,1,0:T(8,128)(2,1)}, bf16[3,3,192,576]{3,2,1,0:T(8,128)(2,1)S(1)}, u32[]{:S(2)}) %copy-start.4) | copy-done | bytes 1990680
  25.1 10.4 %all-to-all-done = bf16[64,2,1536]{2,1,0:T(2,128)(2,1)S(1)} async-done(((bf16[64,2,1536]{2,1,0:T(2,128)(2,1)}), bf16[64,2,1536]{2,1,0:T(2,128)(2,1)S(1)}, u32[]{:S(2)}, u32[]{:S(2)}) %all-to-all-start) | async-done | bytes 393248 | tf_op jit(solution)/shard_map/all_to_all | solution.py:274
  35.5 0.2 copy.11
  35.8 3.3 %collective-permute-start = (bf16[2,64,1536]{2,1,0:T(8,128)(2,1)S(1)}, bf16[2,64,1536]{2,1,0:T(8,128)(2,1)S(1)}, u32[]{:S(2)}, u32[]{:S(2)}) collective-permute-start(bf16[2,64,1536]{2,1,0:T(8,128)(2,1)S(1)} %bitcast.21), channel_id=1, source_target_pairs={{0,64},{64,128},{128,192},{192,256},{256,320},{320,384},{384,448},... | collective-permute-start | bytes 1179656 | tf_op jit(solution)/shard_map/ppermute | solution.py:24
  39.1 2.4 %all-gather.1 = bf16[4,64,1536]{2,1,0:T(8,128)(2,1)S(1)} all-gather(bf16[2,64,1536]{2,1,0:T(8,128)(2,1)S(1)} %bitcast.22), channel_id=3, replica_groups=mesh['tm'=8,'chip'=32,'core'=2] {'core'}, dimensions={0}, use_global_device_ids=true | all-gather | bytes 1179648 | tf_op jit(solution)/shard_map/all_gather | solution.py:280
  41.4 0.0 copy-done.1
  41.4 0.0 copy-done.8
  41.4 0.0 copy-start.5
  41.4 1.6 %copy-done.5 = bf16[3,3,192,576]{3,2,1,0:T(8,128)(2,1)S(1)} copy-done((bf16[3,3,192,576]{3,2,1,0:T(8,128)(2,1)S(1)}, bf16[3,3,192,576]{3,2,1,0:T(8,128)(2,1)}, u32[]{:S(2)}) %copy-start.5) | copy-done | bytes 1990680
  43.1 0.0 copy-start.3
  43.1 0.0 copy-start.6
  43.1 0.0 copy-start.9
  43.1 2.3 %shard_map.75 = (f32[2,4,64,192]{3,2,1,0:T(8,128)S(1)}, f32[2,4,64,192]{3,2,1,0:T(8,128)S(1)}) custom-call(bf16[2,2,64,1536]{3,2,1,0:T(8,128)(2,1)S(1)} %bitcast.13, f32[1,192]{1,0:T(1,128)S(1)} %bitcast.16, bf16[3,3,3,192,192]{4,3,2,1,0:T(8,128)(2,1)S(1)} %copy-done.1, bf16[3,3,192,576]{3,2,1,0:T(8,128)(2,1)S(1)} %copy-done.5), custom_call_target="tpu_custom_call" | custom-call | flops 1019215872 | bytes 4194304 | tf_op jit(solution)/shard_map/pallas_call | solution.py:248
  45.4 0.0 collective-permute-done
  45.4 3.2 %all-gather = bf16[4,64,1536]{2,1,0:T(8,128)(2,1)S(1)} all-gather(bf16[2,64,1536]{2,1,0:T(8,128)(2,1)S(1)} %collective-permute-done), channel_id=2, replica_groups=mesh['tm'=8,'chip'=32,'core'=2] {'core'}, dimensions={0}, use_global_device_ids=true | all-gather | bytes 1179648 | tf_op jit(solution)/shard_map/all_gather | solution.py:287
  48.7 0.0 copy-done.3
  48.7 0.0 copy-done.6
  48.7 0.0 copy-done.9
  48.7 3.5 %shard_map.76 = (bf16[2,64,768]{2,1,0:T(8,128)(2,1)S(1)}, bf16[2,64,384]{2,1,0:T(8,128)(2,1)S(1)}) custom-call(bf16[2,2,64,1536]{3,2,1,0:T(8,128)(2,1)S(1)} %bitcast.15, f32[2,4,64,192]{3,2,1,0:T(8,128)S(1)} %get-tuple-element.22.z_part, f32[2,4,64,192]{3,2,1,0:T(8,128)S(1)} %get-tuple-element.23.d_part, bf16[3,3,192,576]{3,2,1,0:T(8,128)(2,1)S(1)} %copy-done.6, ...), custom_call_target="tpu_custom_call" | custom-call | flops 1019215872 | bytes 4194304 | tf_op jit(solution)/shard_map/pallas_call | solution.py:248
  52.2 1.9 %collective-permute-start.1 = (bf16[2,64,384]{2,1,0:T(8,128)(2,1)S(1)}, bf16[2,64,384]{2,1,0:T(8,128)(2,1)S(1)}, u32[]{:S(2)}, u32[]{:S(2)}) collective-permute-start(bf16[2,64,384]{2,1,0:T(8,128)(2,1)S(1)} %get-tuple-element.25), channel_id=1, source_target_pairs={{64,0},{128,64},{192,128},{256,192},{320,256},{384,320},{448,384},... | collective-permute-start | bytes 294920 | tf_op jit(solution)/shard_map/ppermute | solution.py:17
  54.1 1.2 %shard_map.77 = (f32[2,64,384]{2,1,0:T(8,128)S(1)}, f32[2,64,384]{2,1,0:T(8,128)S(1)}, f32[2,64,384]{2,1,0:T(8,128)S(1)}, f32[2,64,384]{2,1,0:T(8,128)S(1)}) custom-call(bf16[2,2,64,1536]{3,2,1,0:T(8,128)(2,1)S(1)} %bitcast.14, bf16[2,64,768]{2,1,0:T(8,128)(2,1)S(1)} %get-tuple-element.26.d_own, bf16[3,3,192,576]{3,2,1,0:T(8,128)(2,1)S(1)} %copy-done.3, ...), custom_call_target="tpu_custom_call" | custom-call | flops 254803968 | bytes 4194304 | tf_op jit(solution)/shard_map/pallas_call | solution.py:248
  55.3 6.0 %collective-permute-done.1.late = bf16[2,64,384]{2,1,0:T(8,128)(2,1)S(1)} collective-permute-done((bf16[2,64,384]{2,1,0:T(8,128)(2,1)S(1)}, bf16[2,64,384]{2,1,0:T(8,128)(2,1)S(1)}, u32[]{:S(2)}, u32[]{:S(2)}) %collective-permute-start.1) | collective-permute-done | bytes 98336 | tf_op jit(solution)/shard_map/ppermute | solution.py:17
  61.3 0.8 %shard_map.78 = bf16[2,64,384]{2,1,0:T(8,128)(2,1)} custom-call(bf16[2,64,384]{2,1,0:T(8,128)(2,1)S(1)} %collective-permute-done.1.late, f32[2,64,384]{2,1,0:T(8,128)S(1)} %get-tuple-element.27.base, f32[2,64,384]{2,1,0:T(8,128)S(1)} %get-tuple-element.28.slope, f32[2,64,384]{2,1,0:T(8,128)S(1)} %get-tuple-element.29.along, ...), custom_call_target="tpu_custom_call" | custom-call | flops 42467328 | bytes 4194304 | tf_op jit(solution)/shard_map/pallas_call | solution.py:248
Async XLA Ops:
  1.7 33.8 %all-to-all-start = ((bf16[64,2,1536]{2,1,0:T(2,128)(2,1)}), bf16[64,2,1536]{2,1,0:T(2,128)(2,1)S(1)}, u32[]{:S(2)}, u32[]{:S(2)}) async-start(bf16[64,2,1536]{2,1,0:T(2,128)(2,1)} %bitcast.23), calls=%async_computation | async-start | bytes 786432 | tf_op jit(solution)/shard_map/all_to_all | solution.py:274
  18.3 1.8 %copy-start = (bf16[3,3,3,192,192]{4,3,2,1,0:T(8,128)(2,1)S(1)}, bf16[3,3,3,192,192]{4,3,2,1,0:T(8,128)(2,1)}, u32[]{:S(2)}) copy-start(bf16[3,3,3,192,192]{4,3,2,1,0:T(8,128)(2,1)} %conv_one.5) | copy-start | bytes 5971972
  20.1 1.7 %copy-start.7 = (bf16[3,3,3,192,192]{4,3,2,1,0:T(8,128)(2,1)S(1)}, bf16[3,3,3,192,192]{4,3,2,1,0:T(8,128)(2,1)}, u32[]{:S(2)}) copy-start(bf16[3,3,3,192,192]{4,3,2,1,0:T(8,128)(2,1)} %conv_two.1) | copy-start | bytes 5971972
  21.8 19.6 %copy-start.1 = (bf16[3,3,3,192,192]{4,3,2,1,0:T(8,128)(2,1)S(1)}, bf16[3,3,3,192,192]{4,3,2,1,0:T(8,128)(2,1)}, u32[]{:S(2)}) copy-start(bf16[3,3,3,192,192]{4,3,2,1,0:T(8,128)(2,1)} %conv_one.5) | copy-start | bytes 5971972
  21.8 19.6 %copy-start.8 = (f32[192]{0:T(256)S(1)}, f32[192]{0:T(256)}, u32[]{:S(2)}) copy-start(f32[192]{0:T(256)} %param.10) | copy-start | bytes 2308
  22.4 1.3 %copy-start.2 = (bf16[3,3,192,576]{3,2,1,0:T(8,128)(2,1)}, bf16[3,3,192,576]{3,2,1,0:T(8,128)(2,1)S(1)}, u32[]{:S(2)}) copy-start(bf16[3,3,192,576]{3,2,1,0:T(8,128)(2,1)S(1)} %get-tuple-element.24.one) | copy-start | bytes 5971972
  23.8 1.4 %copy-start.4 = (bf16[3,3,192,576]{3,2,1,0:T(8,128)(2,1)}, bf16[3,3,192,576]{3,2,1,0:T(8,128)(2,1)S(1)}, u32[]{:S(2)}) copy-start(bf16[3,3,192,576]{3,2,1,0:T(8,128)(2,1)S(1)} %get-tuple-element.21.turned.two) | copy-start | bytes 5971972
  35.8 9.7 %collective-permute-start = (bf16[2,64,1536]{2,1,0:T(8,128)(2,1)S(1)}, bf16[2,64,1536]{2,1,0:T(8,128)(2,1)S(1)}, u32[]{:S(2)}, u32[]{:S(2)}) collective-permute-start(bf16[2,64,1536]{2,1,0:T(8,128)(2,1)S(1)} %bitcast.21), channel_id=1, source_target_pairs={{0,64},{64,128},{128,192},{192,256},{256,320},{320,384},{384,448},... | collective-permute-start | bytes 1179656 | tf_op jit(solution)/shard_map/ppermute | solution.py:24
  41.4 1.6 %copy-start.5 = (bf16[3,3,192,576]{3,2,1,0:T(8,128)(2,1)S(1)}, bf16[3,3,192,576]{3,2,1,0:T(8,128)(2,1)}, u32[]{:S(2)}) copy-start(bf16[3,3,192,576]{3,2,1,0:T(8,128)(2,1)} %copy-done.4) | copy-start | bytes 5971972
  43.1 5.6 %copy-start.3 = (bf16[3,3,192,576]{3,2,1,0:T(8,128)(2,1)S(1)}, bf16[3,3,192,576]{3,2,1,0:T(8,128)(2,1)}, u32[]{:S(2)}) copy-start(bf16[3,3,192,576]{3,2,1,0:T(8,128)(2,1)} %copy-done.2) | copy-start | bytes 5971972
  43.1 5.6 %copy-start.6 = (bf16[3,3,192,576]{3,2,1,0:T(8,128)(2,1)S(1)}, bf16[3,3,192,576]{3,2,1,0:T(8,128)(2,1)}, u32[]{:S(2)}) copy-start(bf16[3,3,192,576]{3,2,1,0:T(8,128)(2,1)} %copy-done.4) | copy-start | bytes 5971972
  43.1 5.6 %copy-start.9 = (f32[192]{0:T(256)S(1)}, f32[192]{0:T(256)}, u32[]{:S(2)}) copy-start(f32[192]{0:T(256)} %param.12) | copy-start | bytes 2308
  52.2 9.1 %collective-permute-start.1 = (bf16[2,64,384]{2,1,0:T(8,128)(2,1)S(1)}, bf16[2,64,384]{2,1,0:T(8,128)(2,1)S(1)}, u32[]{:S(2)}, u32[]{:S(2)}) collective-permute-start(bf16[2,64,384]{2,1,0:T(8,128)(2,1)S(1)} %get-tuple-element.25), channel_id=1, source_target_pairs={{64,0},{128,64},{192,128},{256,192},{320,256},{384,320},{448,384},... | collective-permute-start | bytes 294920 | tf_op jit(solution)/shard_map/ppermute | solution.py:17

commit v2 on v1

--- a/solution.py
+++ b/solution.py
@@ -17,10 +17,20 @@
     return lax.ppermute(value, axis, [(source, source + steps) for source in range(first, last)])
 
 
+def x_core(block, count):
+    return jnp.where(block == count // 2 - 1, 1, 0)
+
+
+def x_core_other(block, count):
+    return jnp.where(block == count // 2, 1, 0)
+
+
 def spread(value):
     count = lax.axis_size("tm")
-    later = [(2 * k, 2 * k + 2) for k in range(count - 1)]
-    earlier = [(2 * k + 3, 2 * k + 1) for k in range(count - 1)]
+    here = [1 if k == count // 2 - 1 else 0 for k in range(count)]
+    there = [1 if k == count // 2 else 0 for k in range(count)]
+    later = [(2 * k + here[k], 2 * k + 2 + there[k + 1]) for k in range(count - 1)]
+    earlier = [(2 * k + 3 - here[k + 1], 2 * k + 1 - there[k]) for k in range(count - 1)]
     return lax.ppermute(value, ("tm", "core"), later + earlier)
 
 
@@ -34,7 +44,7 @@
     for move in moves:
         move.start()
 
-    def lay(src, blocks, kind):
+    def lay(src, blocks, core, kind):
         none = jnp.zeros((frames, pair), BF16)
         blocks[0, :, :pair] = none
         blocks[chips - 1, :, 3 * pair :] = none
@@ -42,29 +52,29 @@
             first, last = max(0, 2 * q - 1), min(2 * chips, 2 * q + 3)
             skip = first - (2 * q - 1)
             blocks[q, :, skip * pair : (skip + last - first) * pair] = src[:, first * pair : last * pair]
-        move = pltpu.make_async_copy(blocks, out.at[:, kind], sems.at[3 + kind])
+        move = pltpu.make_async_copy(blocks, out.at[:, core], sems.at[3 + kind])
         move.start()
         return move
 
+    first = x_core(lax.axis_index("tm"), lax.axis_size("tm"))
     moves[0].wait()
-    x_move = lay(x_here, x_blocks, 0)
+    x_move = lay(x_here, x_blocks, first, 0)
     moves[1].wait()
     moves[2].wait()
     at = lax.broadcasted_iota(jnp.int32, dy.shape, 0)
     factor = jnp.where(at == 0, scale[0].astype(F32), scale[1].astype(F32)).astype(BF16)
     dy[...] = dy[...] * factor
-    dy_move = lay(dy, dy_blocks, 1)
+    dy_move = lay(dy, dy_blocks, 1 - first, 1)
     x_move.wait()
     dy_move.wait()
 
 
-def turn_kernel(conv_one, conv_two, one, two):
-    width = conv_one.shape[-1]
-    for src, dst in ((conv_two, two), (conv_one, one)):
-        for a in range(3):
-            for b in range(3):
-                for e in range(3):
-                    dst[a, b, :, e * width : (e + 1) * width] = src[2 - a, 2 - b, 2 - e]
+def turn_kernel(src, dst):
+    width = src.shape[-1]
+    for a in range(3):
+        for b in range(3):
+            for e in range(3):
+                dst[a, b, :, e * width : (e + 1) * width] = src[2 - a, 2 - b, 2 - e]
 
 
 def lefts(field, columns, width):
@@ -129,14 +139,14 @@
     return left, right, first
 
 
-def hidden(core, src, gain, hid):
+def hidden(core, kind, src, gain, hid):
     width = gain.shape[-1]
     part = 2 * width // 3
     gains = thirds(jnp.concatenate([gain, gain], axis=1))
     for frame in range(2):
         for p in range(3):
             lanes = pl.ds(pl.multiple_of((p + core) * 2 * width, 2 * width), 2 * width)
-            value = src[0, frame, :, lanes].astype(F32)
+            value = src[kind, frame, :, lanes].astype(F32)
             left, right, first = two_sums(value * value)
             left, right = (0.5 * lax.rsqrt(total * (1.0 / width) + EPS) for total in (left, right))
             scales = left, jnp.where(first, left, right), right
@@ -146,16 +156,16 @@
                 hid[frame, :, at : at + part] = (h + h * jnp.tanh(h)).astype(BF16)
 
 
-def fields_of(core, src, gain, hid):
+def fields_of(core, kind, src, gain, hid):
     width = gain.shape[-1]
-    hidden(core, src, gain, hid)
+    hidden(core, kind, src, gain, hid)
     lanes = pl.ds(pl.multiple_of(core * 2 * width, 2 * width), 6 * width)
-    return [lefts(hid[f], 4, width) for f in range(2)], [lefts(src[1, f, :, lanes], 4, width) for f in range(2)]
+    return [lefts(hid[f], 4, width) for f in range(2)], [lefts(src[1 - kind, f, :, lanes], 4, width) for f in range(2)]
 
 
 def own_kernel(own, gain_one, conv_one, turned, z_part, d_part, hid):
     rows = own.shape[2]
-    xs, gs = fields_of(lax.axis_index("core"), own, gain_one[...], hid)
+    xs, gs = fields_of(lax.axis_index("core"), x_core(lax.axis_index("tm"), lax.axis_size("tm")), own, gain_one[...], hid)
     for t, terms in enumerate(([(2, xs[0])], [(1, xs[0]), (2, xs[1])])):
         for c, block in enumerate(conv_sum(terms, conv_one, False, rows)):
             z_part[t, c] = block
@@ -169,7 +179,7 @@
 ):
     width = gain_one.shape[-1]
     rows = other.shape[2]
-    xs, gs = fields_of(lax.axis_index("core"), other, gain_one[...], hid)
+    xs, gs = fields_of(lax.axis_index("core"), x_core_other(lax.axis_index("tm"), lax.axis_size("tm")), other, gain_one[...], hid)
     for t, terms in enumerate(([(0, xs[0]), (1, xs[1])], [(0, xs[1])])):
         for c, block in enumerate(conv_sum(terms, conv_one, False, rows)):
             z_all[t, c] = z_part[t, c] + block
@@ -214,8 +224,9 @@
             d_all[t, :, c * width : (c + 1) * width] = block
     lanes = pl.ds(pl.multiple_of((1 + lax.axis_index("core")) * 2 * width, 2 * width), 2 * width)
     gain = jnp.concatenate([gain_one[...]] * 2, axis=1)
+    kind = x_core(lax.axis_index("tm"), lax.axis_size("tm"))
     for t in range(2):
-        value = own[0, t, :, lanes].astype(F32)
+        value = own[kind, t, :, lanes].astype(F32)
         scale = lax.rsqrt(halves(value * value) * (1.0 / width) + EPS)
         normed = value * scale
         h = normed * (0.5 * gain)
@@ -226,7 +237,7 @@
         across[t] = turn * normed
         grad = d_all[t]
         total = halves(across[t] * grad)
-        base[t] = own[1, t, :, lanes].astype(F32) + slope[t] * grad - along[t] * total
+        base[t] = own[1 - kind, t, :, lanes].astype(F32) + slope[t] * grad - along[t] * total
 
 
 def last_kernel(late, base, slope, along, across, out, natural):
@@ -274,10 +285,11 @@
     held = lax.all_to_all(blocks, ("chip", "core"), 0, 0)
     held = held.reshape(tiles // 8, 8, frames, wide).transpose(2, 1, 0, 3).reshape(frames, tiles, wide)
     turned = array((3, 3, width, 3 * width), BF16)
-    turned_one, turned_two = call(turn_kernel, "vv", (turned, turned), [], 10**9, conv_one, conv_two)
-    held, turned_one, turned_two = lax.optimization_barrier((held, turned_one, turned_two))
+    turned_two = call(turn_kernel, "v", turned, [], 10**9, conv_two)
+    held, turned_two = lax.optimization_barrier((held, turned_two))
     arrived = spread(held)
     own = lax.all_gather(held, "core")
+    turned_one = call(turn_kernel, "v", turned, [], 10**9, conv_one)
     sums = (frames, 4, tiles, width)
     hid = pltpu.VMEM((frames, tiles, 6 * width), BF16)
     z_part, d_part = call(

time: 62.4 us -> 62.4 us (level)
  waiting for transfers between devices: 16.4 us -> 21.4 us
  local copies, waits for them, and re-layouts: 8.07 us -> 3.35 us
    unnamed x20 -> x12, local copies, waits for them, and re-layouts: 7.85 us -> 3.13 us
    all_to_all x1, waiting for transfers between devices: 10.4 us -> 13.8 us  [body(): held = lax.all_to_all(blocks, ('chip', 'core'), 0, 0)]
    ppermute x1, waiting for transfers between devices: 0.04 us -> 1.7 us  [spread(): return lax.ppermute(value, ('tm', 'core'), later + earlier)]
    pallas_call x6 -> x7, Pallas kernels: 10.1 us -> 10.1 us  [call(): pl.pallas_call(kernel, out_shape=outs, in_specs=[pl.BlockSpec(memory_spac...]
  transfers between devices with their start and end apart: 3 -> 3, of which waited for: 2 -> 3; matrix products, arithmetic and copies ran while one was open for 0% -> 0% of each run, Pallas kernels for 7% -> 7%
where the time goes in v2:
time: 62.4 us; the launch traced here: 62.1 us
  waiting for transfers between devices  21.4 us (34%)
  starting transfers between devices  21.3 us (34%)
  Pallas kernels  10.1 us (16%)
  blocking collectives  5.92 us (9%)
  local copies, waits for them, and re-layouts  3.35 us (5%)
    all_to_all x1, starting transfers between devices, body(): held = lax.all_to_all(blocks, ('chip', 'core'), 0, 0)  16.6 us
    all_to_all x1, waiting for transfers between devices, body(): held = lax.all_to_all(blocks, ('chip', 'core'), 0, 0)  13.8 us
    pallas_call x7, Pallas kernels, call(): pl.pallas_call(kernel, out_shape=outs, in_specs=[pl.BlockSpec(memory_spac...  10.1 us
    ppermute x1, waiting for transfers between devices, shifted(): lax.ppermute(value, axis, [(source, source + steps) for source in range(f...  5.94 us
    all_gather x1, blocking collectives, body(): other = lax.all_gather(arrived, 'core')  3.25 us
    unnamed x12, local copies, waits for them, and re-layouts  3.13 us
    ppermute x1, starting transfers between devices, spread(): return lax.ppermute(value, ('tm', 'core'), later + earlier)  2.77 us
    all_gather x1, blocking collectives, body(): own = lax.all_gather(held, 'core')  2.67 us
  transfers between devices with their start and end apart: 3, of which 3 were waited for; matrix products, arithmetic and copies ran while one was open for 0% of the time, Pallas kernels for 7%

profile of v2, /device:TPU:6, one launch (start us, length us, event | category | flops | bytes accessed | tf_op | source)
XLA Modules:
  0.0 62.1 jit_solution(15432153730836521125)
XLA Ops:
  0.0 1.7 %shard_map.73 = bf16[32,2,2,1536]{3,2,1,0:T(2,128)(2,1)} custom-call(s32[2]{0:T(128)} %weight.1, bf16[2,24576]{1,0:T(2,128)(2,1)} %bitcast.24, bf16[2,24576]{1,0:T(2,128)(2,1)} %bitcast.25), custom_call_target="tpu_custom_call" | custom-call | flops 1000000 | bytes 4194304 | tf_op jit(solution)/shard_map/pallas_call | solution.py:259
  1.7 16.6 %all-to-all-start = ((bf16[64,2,1536]{2,1,0:T(2,128)(2,1)}), bf16[64,2,1536]{2,1,0:T(2,128)(2,1)S(1)}, u32[]{:S(2)}, u32[]{:S(2)}) async-start(bf16[64,2,1536]{2,1,0:T(2,128)(2,1)} %bitcast.23), calls=%async_computation | async-start | bytes 786432 | tf_op jit(solution)/shard_map/all_to_all | solution.py:285
  18.3 0.0 copy-start.3
  18.3 1.7 %copy-done.3 = bf16[3,3,3,192,192]{4,3,2,1,0:T(8,128)(2,1)S(1)} copy-done((bf16[3,3,3,192,192]{4,3,2,1,0:T(8,128)(2,1)S(1)}, bf16[3,3,3,192,192]{4,3,2,1,0:T(8,128)(2,1)}, u32[]{:S(2)}) %copy-start.3) | copy-done | bytes 1990680
  20.1 0.0 copy-start
  20.1 0.3 shard_map.74.turned.two
  20.4 0.0 copy-start.1
  20.4 1.4 %copy-done.1 = bf16[3,3,192,576]{3,2,1,0:T(8,128)(2,1)} copy-done((bf16[3,3,192,576]{3,2,1,0:T(8,128)(2,1)}, bf16[3,3,192,576]{3,2,1,0:T(8,128)(2,1)S(1)}, u32[]{:S(2)}) %copy-start.1) | copy-done | bytes 1990680
  21.8 13.8 %all-to-all-done = bf16[64,2,1536]{2,1,0:T(2,128)(2,1)S(1)} async-done(((bf16[64,2,1536]{2,1,0:T(2,128)(2,1)}), bf16[64,2,1536]{2,1,0:T(2,128)(2,1)S(1)}, u32[]{:S(2)}, u32[]{:S(2)}) %all-to-all-start) | async-done | bytes 393248 | tf_op jit(solution)/shard_map/all_to_all | solution.py:285
  35.5 0.2 copy.11
  35.8 0.0 copy-start.2
  35.8 0.0 copy-start.4
  35.8 2.8 %collective-permute-start = (bf16[2,64,1536]{2,1,0:T(8,128)(2,1)S(1)}, bf16[2,64,1536]{2,1,0:T(8,128)(2,1)S(1)}, u32[]{:S(2)}, u32[]{:S(2)}) collective-permute-start(bf16[2,64,1536]{2,1,0:T(8,128)(2,1)S(1)} %bitcast.21), channel_id=1, source_target_pairs={{0,64},{64,128},{128,192},{193,257},{256,320},{320,384},{384,448},... | collective-permute-start | bytes 1179656 | tf_op jit(solution)/shard_map/ppermute | solution.py:34
  38.6 0.0 copy-done
  38.6 0.3 shard_map.76.one
  38.9 2.7 %all-gather.1 = bf16[4,64,1536]{2,1,0:T(8,128)(2,1)S(1)} all-gather(bf16[2,64,1536]{2,1,0:T(8,128)(2,1)S(1)} %bitcast.22), channel_id=3, replica_groups=mesh['tm'=8,'chip'=32,'core'=2] {'core'}, dimensions={0}, use_global_device_ids=true | all-gather | bytes 1179648 | tf_op jit(solution)/shard_map/all_gather | solution.py:291
  41.6 0.0 copy-done.2
  41.6 0.0 copy-done.4
  41.6 0.0 copy-start.5
  41.6 2.3 %shard_map.75 = (f32[2,4,64,192]{3,2,1,0:T(8,128)S(1)}, f32[2,4,64,192]{3,2,1,0:T(8,128)S(1)}) custom-call(bf16[2,2,64,1536]{3,2,1,0:T(8,128)(2,1)S(1)} %bitcast.13, f32[1,192]{1,0:T(1,128)S(1)} %bitcast.16, bf16[3,3,3,192,192]{4,3,2,1,0:T(8,128)(2,1)S(1)} %copy-done, bf16[3,3,192,576]{3,2,1,0:T(8,128)(2,1)S(1)} %copy-done.2), custom_call_target="tpu_custom_call" | custom-call | flops 1019215872 | bytes 4194304 | tf_op jit(solution)/shard_map/pallas_call | solution.py:259
  43.9 1.7 %collective-permute-done = bf16[2,64,1536]{2,1,0:T(8,128)(2,1)S(1)} collective-permute-done((bf16[2,64,1536]{2,1,0:T(8,128)(2,1)S(1)}, bf16[2,64,1536]{2,1,0:T(8,128)(2,1)S(1)}, u32[]{:S(2)}, u32[]{:S(2)}) %collective-permute-start) | collective-permute-done | bytes 393248 | tf_op jit(solution)/shard_map/ppermute | solution.py:34
  45.6 3.2 %all-gather = bf16[4,64,1536]{2,1,0:T(8,128)(2,1)S(1)} all-gather(bf16[2,64,1536]{2,1,0:T(8,128)(2,1)S(1)} %collective-permute-done), channel_id=2, replica_groups=mesh['tm'=8,'chip'=32,'core'=2] {'core'}, dimensions={0}, use_global_device_ids=true | all-gather | bytes 1179648 | tf_op jit(solution)/shard_map/all_gather | solution.py:299
  48.8 0.0 copy-done.5
  48.8 3.4 %shard_map.77 = (bf16[2,64,768]{2,1,0:T(8,128)(2,1)S(1)}, bf16[2,64,384]{2,1,0:T(8,128)(2,1)S(1)}) custom-call(bf16[2,2,64,1536]{3,2,1,0:T(8,128)(2,1)S(1)} %bitcast.15, f32[2,4,64,192]{3,2,1,0:T(8,128)S(1)} %get-tuple-element.17.z_part, f32[2,4,64,192]{3,2,1,0:T(8,128)S(1)} %get-tuple-element.18.d_part, bf16[3,3,192,576]{3,2,1,0:T(8,128)(2,1)S(1)} %copy-done.2, ...), custom_call_target="tpu_custom_call" | custom-call | flops 1019215872 | bytes 4194304 | tf_op jit(solution)/shard_map/pallas_call | solution.py:259
  52.3 1.9 %collective-permute-start.1 = (bf16[2,64,384]{2,1,0:T(8,128)(2,1)S(1)}, bf16[2,64,384]{2,1,0:T(8,128)(2,1)S(1)}, u32[]{:S(2)}, u32[]{:S(2)}) collective-permute-start(bf16[2,64,384]{2,1,0:T(8,128)(2,1)S(1)} %get-tuple-element.19), channel_id=1, source_target_pairs={{64,0},{128,64},{192,128},{256,192},{320,256},{384,320},{448,384},... | collective-permute-start | bytes 294920 | tf_op jit(solution)/shard_map/ppermute | solution.py:17
  54.2 1.2 %shard_map.78 = (f32[2,64,384]{2,1,0:T(8,128)S(1)}, f32[2,64,384]{2,1,0:T(8,128)S(1)}, f32[2,64,384]{2,1,0:T(8,128)S(1)}, f32[2,64,384]{2,1,0:T(8,128)S(1)}) custom-call(bf16[2,2,64,1536]{3,2,1,0:T(8,128)(2,1)S(1)} %bitcast.14, bf16[2,64,768]{2,1,0:T(8,128)(2,1)S(1)} %get-tuple-element.20.d_own, bf16[3,3,192,576]{3,2,1,0:T(8,128)(2,1)S(1)} %shard_map.76.one, ...), custom_call_target="tpu_custom_call" | custom-call | flops 254803968 | bytes 4194304 | tf_op jit(solution)/shard_map/pallas_call | solution.py:259
  55.4 5.9 %collective-permute-done.1.late = bf16[2,64,384]{2,1,0:T(8,128)(2,1)S(1)} collective-permute-done((bf16[2,64,384]{2,1,0:T(8,128)(2,1)S(1)}, bf16[2,64,384]{2,1,0:T(8,128)(2,1)S(1)}, u32[]{:S(2)}, u32[]{:S(2)}) %collective-permute-start.1) | collective-permute-done | bytes 98336 | tf_op jit(solution)/shard_map/ppermute | solution.py:17
  61.4 0.8 %shard_map.79 = bf16[2,64,384]{2,1,0:T(8,128)(2,1)} custom-call(bf16[2,64,384]{2,1,0:T(8,128)(2,1)S(1)} %collective-permute-done.1.late, f32[2,64,384]{2,1,0:T(8,128)S(1)} %get-tuple-element.21.base, f32[2,64,384]{2,1,0:T(8,128)S(1)} %get-tuple-element.22.slope, f32[2,64,384]{2,1,0:T(8,128)S(1)} %get-tuple-element.23.along, ...), custom_call_target="tpu_custom_call" | custom-call | flops 42467328 | bytes 4194304 | tf_op jit(solution)/shard_map/pallas_call | solution.py:259
Async XLA Ops:
  1.7 33.8 %all-to-all-start = ((bf16[64,2,1536]{2,1,0:T(2,128)(2,1)}), bf16[64,2,1536]{2,1,0:T(2,128)(2,1)S(1)}, u32[]{:S(2)}, u32[]{:S(2)}) async-start(bf16[64,2,1536]{2,1,0:T(2,128)(2,1)} %bitcast.23), calls=%async_computation | async-start | bytes 786432 | tf_op jit(solution)/shard_map/all_to_all | solution.py:285
  18.3 1.8 %copy-start.3 = (bf16[3,3,3,192,192]{4,3,2,1,0:T(8,128)(2,1)S(1)}, bf16[3,3,3,192,192]{4,3,2,1,0:T(8,128)(2,1)}, u32[]{:S(2)}) copy-start(bf16[3,3,3,192,192]{4,3,2,1,0:T(8,128)(2,1)} %src.2) | copy-start | bytes 5971972
  20.1 18.5 %copy-start = (bf16[3,3,3,192,192]{4,3,2,1,0:T(8,128)(2,1)S(1)}, bf16[3,3,3,192,192]{4,3,2,1,0:T(8,128)(2,1)}, u32[]{:S(2)}) copy-start(bf16[3,3,3,192,192]{4,3,2,1,0:T(8,128)(2,1)} %conv_one.3) | copy-start | bytes 5971972
  20.4 1.4 %copy-start.1 = (bf16[3,3,192,576]{3,2,1,0:T(8,128)(2,1)}, bf16[3,3,192,576]{3,2,1,0:T(8,128)(2,1)S(1)}, u32[]{:S(2)}) copy-start(bf16[3,3,192,576]{3,2,1,0:T(8,128)(2,1)S(1)} %shard_map.74.turned.two) | copy-start | bytes 5971972
  35.8 5.8 %copy-start.2 = (bf16[3,3,192,576]{3,2,1,0:T(8,128)(2,1)S(1)}, bf16[3,3,192,576]{3,2,1,0:T(8,128)(2,1)}, u32[]{:S(2)}) copy-start(bf16[3,3,192,576]{3,2,1,0:T(8,128)(2,1)} %copy-done.1) | copy-start | bytes 5971972
  35.8 5.8 %copy-start.4 = (f32[192]{0:T(256)S(1)}, f32[192]{0:T(256)}, u32[]{:S(2)}) copy-start(f32[192]{0:T(256)} %param.10) | copy-start | bytes 2308
  35.8 9.8 %collective-permute-start = (bf16[2,64,1536]{2,1,0:T(8,128)(2,1)S(1)}, bf16[2,64,1536]{2,1,0:T(8,128)(2,1)S(1)}, u32[]{:S(2)}, u32[]{:S(2)}) collective-permute-start(bf16[2,64,1536]{2,1,0:T(8,128)(2,1)S(1)} %bitcast.21), channel_id=1, source_target_pairs={{0,64},{64,128},{128,192},{193,257},{256,320},{320,384},{384,448},... | collective-permute-start | bytes 1179656 | tf_op jit(solution)/shard_map/ppermute | solution.py:34
  41.6 7.3 %copy-start.5 = (f32[192]{0:T(256)S(1)}, f32[192]{0:T(256)}, u32[]{:S(2)}) copy-start(f32[192]{0:T(256)} %param.12) | copy-start | bytes 2308
  52.3 9.1 %collective-permute-start.1 = (bf16[2,64,384]{2,1,0:T(8,128)(2,1)S(1)}, bf16[2,64,384]{2,1,0:T(8,128)(2,1)S(1)}, u32[]{:S(2)}, u32[]{:S(2)}) collective-permute-start(bf16[2,64,384]{2,1,0:T(8,128)(2,1)S(1)} %get-tuple-element.19), channel_id=1, source_target_pairs={{64,0},{128,64},{192,128},{256,192},{320,256},{384,320},{448,384},... | collective-permute-start | bytes 294920 | tf_op jit(solution)/shard_map/ppermute | solution.py:17

commit v3 on v2

--- a/solution.py
+++ b/solution.py
@@ -287,7 +287,7 @@
     turned = array((3, 3, width, 3 * width), BF16)
     turned_two = call(turn_kernel, "v", turned, [], 10**9, conv_two)
     held, turned_two = lax.optimization_barrier((held, turned_two))
-    arrived = spread(held)
+    arrived = jnp.concatenate([spread(held[frame : frame + 1]) for frame in range(frames)], axis=0)
     own = lax.all_gather(held, "core")
     turned_one = call(turn_kernel, "v", turned, [], 10**9, conv_one)
     sums = (frames, 4, tiles, width)

time: 62.4 us -> 64.2 us (1.029)
  waiting for transfers between devices: 21.4 us -> 17.2 us
  local copies, waits for them, and re-layouts: 3.35 us -> 5.59 us
  starting transfers between devices: 21.3 us -> 23.4 us
  blocking collectives: 5.92 us -> 7.29 us
    all_to_all x1, waiting for transfers between devices: 13.8 us -> 11.3 us  [body(): held = lax.all_to_all(blocks, ('chip', 'core'), 0, 0)]
    all_gather x1, blocking collectives: 2.67 us -> 4.92 us  [body(): own = lax.all_gather(held, 'core')]
    unnamed x12 -> x18, local copies, waits for them, and re-layouts: 3.13 us -> 5.34 us
    ppermute x1 -> x2, starting transfers between devices: 2.77 us -> 4.9 us  [spread(): return lax.ppermute(value, ('tm', 'core'), later + earlier)]
    ppermute x1 -> x2, waiting for transfers between devices: 1.7 us -> 0.01 us  [spread(): return lax.ppermute(value, ('tm', 'core'), later + earlier)]
    all_gather x1, blocking collectives: 3.25 us -> 2.37 us  [body(): other = lax.all_gather(arrived, 'core')]
  transfers between devices with their start and end apart: 3 -> 4, of which waited for: 3 -> 2; matrix products, arithmetic and copies ran while one was open for 0% -> 0% of each run, Pallas kernels for 7% -> 6%
where the time goes in v3:
time: 64.2 us; the launch traced here: 63.8 us
  starting transfers between devices  23.4 us (36%)
  waiting for transfers between devices  17.2 us (27%)
  Pallas kernels  10.1 us (16%)
  blocking collectives  7.29 us (11%)
  local copies, waits for them, and re-layouts  5.59 us (9%)
    all_to_all x1, starting transfers between devices, body(): held = lax.all_to_all(blocks, ('chip', 'core'), 0, 0)  16.6 us
    all_to_all x1, waiting for transfers between devices, body(): held = lax.all_to_all(blocks, ('chip', 'core'), 0, 0)  11.3 us
    pallas_call x7, Pallas kernels, call(): pl.pallas_call(kernel, out_shape=outs, in_specs=[pl.BlockSpec(memory_spac...  10.1 us
    ppermute x1, waiting for transfers between devices, shifted(): lax.ppermute(value, axis, [(source, source + steps) for source in range(f...  5.92 us
    unnamed x18, local copies, waits for them, and re-layouts  5.34 us
    all_gather x1, blocking collectives, body(): own = lax.all_gather(held, 'core')  4.92 us
    ppermute x2, starting transfers between devices, spread(): return lax.ppermute(value, ('tm', 'core'), later + earlier)  4.9 us
    all_gather x1, blocking collectives, body(): other = lax.all_gather(arrived, 'core')  2.37 us
  transfers between devices with their start and end apart: 4, of which 2 were waited for; matrix products, arithmetic and copies ran while one was open for 0% of the time, Pallas kernels for 6%

profile of v3, /device:TPU:6, one launch (start us, length us, event | category | flops | bytes accessed | tf_op | source)
XLA Modules:
  0.0 63.8 jit_solution(1783331815258746236)
XLA Ops:
  0.0 1.8 %shard_map.73 = bf16[32,2,2,1536]{3,2,1,0:T(2,128)(2,1)} custom-call(s32[2]{0:T(128)} %weight.1, bf16[2,24576]{1,0:T(2,128)(2,1)} %bitcast.24, bf16[2,24576]{1,0:T(2,128)(2,1)} %bitcast.25), custom_call_target="tpu_custom_call" | custom-call | flops 1000000 | bytes 4194304 | tf_op jit(solution)/shard_map/pallas_call | solution.py:259
  1.8 16.6 %all-to-all-start = ((bf16[64,2,1536]{2,1,0:T(2,128)(2,1)}), bf16[64,2,1536]{2,1,0:T(2,128)(2,1)S(1)}, u32[]{:S(2)}, u32[]{:S(2)}) async-start(bf16[64,2,1536]{2,1,0:T(2,128)(2,1)} %bitcast.23), calls=%async_computation | async-start | bytes 786432 | tf_op jit(solution)/shard_map/all_to_all | solution.py:285
  18.4 0.0 copy-start
  18.4 1.7 %copy-done = bf16[3,3,3,192,192]{4,3,2,1,0:T(8,128)(2,1)S(1)} copy-done((bf16[3,3,3,192,192]{4,3,2,1,0:T(8,128)(2,1)S(1)}, bf16[3,3,3,192,192]{4,3,2,1,0:T(8,128)(2,1)}, u32[]{:S(2)}) %copy-start) | copy-done | bytes 1990680
  20.1 0.0 copy-start.6
  20.1 0.3 shard_map.76.one
  20.4 0.0 copy-start.2
  20.4 1.4 %copy-done.2 = bf16[3,3,192,576]{3,2,1,0:T(8,128)(2,1)} copy-done((bf16[3,3,192,576]{3,2,1,0:T(8,128)(2,1)}, bf16[3,3,192,576]{3,2,1,0:T(8,128)(2,1)S(1)}, u32[]{:S(2)}) %copy-start.2) | copy-done | bytes 1990680
  21.8 0.9 %copy-done.6 = bf16[3,3,3,192,192]{4,3,2,1,0:T(8,128)(2,1)S(1)} copy-done((bf16[3,3,3,192,192]{4,3,2,1,0:T(8,128)(2,1)S(1)}, bf16[3,3,3,192,192]{4,3,2,1,0:T(8,128)(2,1)}, u32[]{:S(2)}) %copy-start.6) | copy-done | bytes 1990680
  22.7 0.0 copy-start.1
  22.7 0.0 copy-start.7
  22.7 0.3 shard_map.74.turned.two
  23.0 0.0 copy-start.4
  23.0 1.3 %copy-done.4 = bf16[3,3,192,576]{3,2,1,0:T(8,128)(2,1)} copy-done((bf16[3,3,192,576]{3,2,1,0:T(8,128)(2,1)}, bf16[3,3,192,576]{3,2,1,0:T(8,128)(2,1)S(1)}, u32[]{:S(2)}) %copy-start.4) | copy-done | bytes 1990680
  24.3 11.3 %all-to-all-done = bf16[64,2,1536]{2,1,0:T(2,128)(2,1)S(1)} async-done(((bf16[64,2,1536]{2,1,0:T(2,128)(2,1)}), bf16[64,2,1536]{2,1,0:T(2,128)(2,1)S(1)}, u32[]{:S(2)}, u32[]{:S(2)}) %all-to-all-start) | async-done | bytes 393248 | tf_op jit(solution)/shard_map/all_to_all | solution.py:285
  35.6 0.0 copy-start.5
  35.6 0.2 copy.11
  35.8 2.7 %collective-permute-start = (bf16[1,64,1536]{2,1,0:T(8,128)(2,1)S(1)}, bf16[1,64,1536]{2,1,0:T(8,128)(2,1)S(1)}, u32[]{:S(2)}, u32[]{:S(2)}) collective-permute-start(bf16[1,64,1536]{2,1,0:T(8,128)(2,1)S(1)} %get-tuple-element.25), channel_id=1, source_target_pairs={{0,64},{64,128},{128,192},{193,257},{256,320},{320,384},{384,448},... | collective-permute-start | bytes 589832 | tf_op jit(solution)/shard_map/ppermute | solution.py:34
  38.6 2.2 %collective-permute-start.1 = (bf16[1,64,1536]{2,1,0:T(8,128)(2,1)S(1)}, bf16[1,64,1536]{2,1,0:T(8,128)(2,1)S(1)}, u32[]{:S(2)}, u32[]{:S(2)}) collective-permute-start(bf16[1,64,1536]{2,1,0:T(8,128)(2,1)S(1)} %get-tuple-element.26), channel_id=1, source_target_pairs={{0,64},{64,128},{128,192},{193,257},{256,320},{320,384},{384,448},... | collective-permute-start | bytes 589832 | tf_op jit(solution)/shard_map/ppermute | solution.py:34
  40.8 4.9 %all-gather.1 = bf16[4,64,1536]{2,1,0:T(8,128)(2,1)S(1)} all-gather(bf16[2,64,1536]{2,1,0:T(8,128)(2,1)S(1)} %bitcast.21), channel_id=3, replica_groups=mesh['tm'=8,'chip'=32,'core'=2] {'core'}, dimensions={0}, use_global_device_ids=true | all-gather | bytes 1179648 | tf_op jit(solution)/shard_map/all_gather | solution.py:291
  45.7 0.0 copy-done.1
  45.7 0.0 copy-done.7
  45.7 0.0 copy-done.5
  45.7 0.0 copy-start.3
  45.7 0.0 copy-start.8
  45.7 2.3 %shard_map.75 = (f32[2,4,64,192]{3,2,1,0:T(8,128)S(1)}, f32[2,4,64,192]{3,2,1,0:T(8,128)S(1)}) custom-call(bf16[2,2,64,1536]{3,2,1,0:T(8,128)(2,1)S(1)} %bitcast.13, f32[1,192]{1,0:T(1,128)S(1)} %bitcast.16, bf16[3,3,3,192,192]{4,3,2,1,0:T(8,128)(2,1)S(1)} %copy-done.1, bf16[3,3,192,576]{3,2,1,0:T(8,128)(2,1)S(1)} %copy-done.5), custom_call_target="tpu_custom_call" | custom-call | flops 1019215872 | bytes 4194304 | tf_op jit(solution)/shard_map/pallas_call | solution.py:259
  48.0 0.0 collective-permute-done
  48.0 0.0 collective-permute-done.1
  48.1 2.4 %all-gather = bf16[4,64,1536]{2,1,0:T(8,128)(2,1)S(1)} all-gather(bf16[2,64,1536]{2,1,0:T(8,128)(2,1)S(1)} %pad_maximum_fusion), channel_id=2, replica_groups=mesh['tm'=8,'chip'=32,'core'=2] {'core'}, dimensions={0}, use_global_device_ids=true | all-gather | bytes 1179648 | tf_op jit(solution)/shard_map/all_gather | solution.py:299
  50.5 0.0 copy-done.3
  50.5 0.0 copy-done.8
  50.5 3.5 %shard_map.77 = (bf16[2,64,768]{2,1,0:T(8,128)(2,1)S(1)}, bf16[2,64,384]{2,1,0:T(8,128)(2,1)S(1)}) custom-call(bf16[2,2,64,1536]{3,2,1,0:T(8,128)(2,1)S(1)} %bitcast.15, f32[2,4,64,192]{3,2,1,0:T(8,128)S(1)} %get-tuple-element.17.z_part, f32[2,4,64,192]{3,2,1,0:T(8,128)S(1)} %get-tuple-element.18.d_part, bf16[3,3,192,576]{3,2,1,0:T(8,128)(2,1)S(1)} %copy-done.5, ...), custom_call_target="tpu_custom_call" | custom-call | flops 1019215872 | bytes 4194304 | tf_op jit(solution)/shard_map/pallas_call | solution.py:259
  54.0 1.9 %collective-permute-start.2 = (bf16[2,64,384]{2,1,0:T(8,128)(2,1)S(1)}, bf16[2,64,384]{2,1,0:T(8,128)(2,1)S(1)}, u32[]{:S(2)}, u32[]{:S(2)}) collective-permute-start(bf16[2,64,384]{2,1,0:T(8,128)(2,1)S(1)} %get-tuple-element.19), channel_id=1, source_target_pairs={{64,0},{128,64},{192,128},{256,192},{320,256},{384,320},{448,384},... | collective-permute-start | bytes 294920 | tf_op jit(solution)/shard_map/ppermute | solution.py:17
  55.9 1.2 %shard_map.78 = (f32[2,64,384]{2,1,0:T(8,128)S(1)}, f32[2,64,384]{2,1,0:T(8,128)S(1)}, f32[2,64,384]{2,1,0:T(8,128)S(1)}, f32[2,64,384]{2,1,0:T(8,128)S(1)}) custom-call(bf16[2,2,64,1536]{3,2,1,0:T(8,128)(2,1)S(1)} %bitcast.14, bf16[2,64,768]{2,1,0:T(8,128)(2,1)S(1)} %get-tuple-element.20.d_own, bf16[3,3,192,576]{3,2,1,0:T(8,128)(2,1)S(1)} %copy-done.3, ...), custom_call_target="tpu_custom_call" | custom-call | flops 254803968 | bytes 4194304 | tf_op jit(solution)/shard_map/pallas_call | solution.py:259
  57.1 5.9 %collective-permute-done.2.late = bf16[2,64,384]{2,1,0:T(8,128)(2,1)S(1)} collective-permute-done((bf16[2,64,384]{2,1,0:T(8,128)(2,1)S(1)}, bf16[2,64,384]{2,1,0:T(8,128)(2,1)S(1)}, u32[]{:S(2)}, u32[]{:S(2)}) %collective-permute-start.2) | collective-permute-done | bytes 98336 | tf_op jit(solution)/shard_map/ppermute | solution.py:17
  63.0 0.8 %shard_map.79 = bf16[2,64,384]{2,1,0:T(8,128)(2,1)} custom-call(bf16[2,64,384]{2,1,0:T(8,128)(2,1)S(1)} %collective-permute-done.2.late, f32[2,64,384]{2,1,0:T(8,128)S(1)} %get-tuple-element.21.base, f32[2,64,384]{2,1,0:T(8,128)S(1)} %get-tuple-element.22.slope, f32[2,64,384]{2,1,0:T(8,128)S(1)} %get-tuple-element.23.along, ...), custom_call_target="tpu_custom_call" | custom-call | flops 42467328 | bytes 4194304 | tf_op jit(solution)/shard_map/pallas_call | solution.py:259
  (2 shorter events, 0.1 us)
Async XLA Ops:
  1.8 33.8 %all-to-all-start = ((bf16[64,2,1536]{2,1,0:T(2,128)(2,1)}), bf16[64,2,1536]{2,1,0:T(2,128)(2,1)S(1)}, u32[]{:S(2)}, u32[]{:S(2)}) async-start(bf16[64,2,1536]{2,1,0:T(2,128)(2,1)} %bitcast.23), calls=%async_computation | async-start | bytes 786432 | tf_op jit(solution)/shard_map/all_to_all | solution.py:285
  18.4 1.8 %copy-start = (bf16[3,3,3,192,192]{4,3,2,1,0:T(8,128)(2,1)S(1)}, bf16[3,3,3,192,192]{4,3,2,1,0:T(8,128)(2,1)}, u32[]{:S(2)}) copy-start(bf16[3,3,3,192,192]{4,3,2,1,0:T(8,128)(2,1)} %conv_one.3) | copy-start | bytes 5971972
  20.1 2.5 %copy-start.6 = (bf16[3,3,3,192,192]{4,3,2,1,0:T(8,128)(2,1)S(1)}, bf16[3,3,3,192,192]{4,3,2,1,0:T(8,128)(2,1)}, u32[]{:S(2)}) copy-start(bf16[3,3,3,192,192]{4,3,2,1,0:T(8,128)(2,1)} %src.2) | copy-start | bytes 5971972
  20.4 1.4 %copy-start.2 = (bf16[3,3,192,576]{3,2,1,0:T(8,128)(2,1)}, bf16[3,3,192,576]{3,2,1,0:T(8,128)(2,1)S(1)}, u32[]{:S(2)}) copy-start(bf16[3,3,192,576]{3,2,1,0:T(8,128)(2,1)S(1)} %shard_map.76.one) | copy-start | bytes 5971972
  22.7 23.0 %copy-start.1 = (bf16[3,3,3,192,192]{4,3,2,1,0:T(8,128)(2,1)S(1)}, bf16[3,3,3,192,192]{4,3,2,1,0:T(8,128)(2,1)}, u32[]{:S(2)}) copy-start(bf16[3,3,3,192,192]{4,3,2,1,0:T(8,128)(2,1)} %conv_one.3) | copy-start | bytes 5971972
  22.7 23.0 %copy-start.7 = (f32[192]{0:T(256)S(1)}, f32[192]{0:T(256)}, u32[]{:S(2)}) copy-start(f32[192]{0:T(256)} %param.10) | copy-start | bytes 2308
  23.0 1.3 %copy-start.4 = (bf16[3,3,192,576]{3,2,1,0:T(8,128)(2,1)}, bf16[3,3,192,576]{3,2,1,0:T(8,128)(2,1)S(1)}, u32[]{:S(2)}) copy-start(bf16[3,3,192,576]{3,2,1,0:T(8,128)(2,1)S(1)} %shard_map.74.turned.two) | copy-start | bytes 5971972
  35.6 10.1 %copy-start.5 = (bf16[3,3,192,576]{3,2,1,0:T(8,128)(2,1)S(1)}, bf16[3,3,192,576]{3,2,1,0:T(8,128)(2,1)}, u32[]{:S(2)}) copy-start(bf16[3,3,192,576]{3,2,1,0:T(8,128)(2,1)} %copy-done.4) | copy-start | bytes 5971972
  35.8 12.2 %collective-permute-start = (bf16[1,64,1536]{2,1,0:T(8,128)(2,1)S(1)}, bf16[1,64,1536]{2,1,0:T(8,128)(2,1)S(1)}, u32[]{:S(2)}, u32[]{:S(2)}) collective-permute-start(bf16[1,64,1536]{2,1,0:T(8,128)(2,1)S(1)} %get-tuple-element.25), channel_id=1, source_target_pairs={{0,64},{64,128},{128,192},{193,257},{256,320},{320,384},{384,448},... | collective-permute-start | bytes 589832 | tf_op jit(solution)/shard_map/ppermute | solution.py:34
  38.6 9.5 %collective-permute-start.1 = (bf16[1,64,1536]{2,1,0:T(8,128)(2,1)S(1)}, bf16[1,64,1536]{2,1,0:T(8,128)(2,1)S(1)}, u32[]{:S(2)}, u32[]{:S(2)}) collective-permute-start(bf16[1,64,1536]{2,1,0:T(8,128)(2,1)S(1)} %get-tuple-element.26), channel_id=1, source_target_pairs={{0,64},{64,128},{128,192},{193,257},{256,320},{320,384},{384,448},... | collective-permute-start | bytes 589832 | tf_op jit(solution)/shard_map/ppermute | solution.py:34
  45.7 4.8 %copy-start.3 = (bf16[3,3,192,576]{3,2,1,0:T(8,128)(2,1)S(1)}, bf16[3,3,192,576]{3,2,1,0:T(8,128)(2,1)}, u32[]{:S(2)}) copy-start(bf16[3,3,192,576]{3,2,1,0:T(8,128)(2,1)} %copy-done.2) | copy-start | bytes 5971972
  45.7 4.8 %copy-start.8 = (f32[192]{0:T(256)S(1)}, f32[192]{0:T(256)}, u32[]{:S(2)}) copy-start(f32[192]{0:T(256)} %param.12) | copy-start | bytes 2308
  54.0 9.1 %collective-permute-start.2 = (bf16[2,64,384]{2,1,0:T(8,128)(2,1)S(1)}, bf16[2,64,384]{2,1,0:T(8,128)(2,1)S(1)}, u32[]{:S(2)}, u32[]{:S(2)}) collective-permute-start(bf16[2,64,384]{2,1,0:T(8,128)(2,1)S(1)} %get-tuple-element.19), channel_id=1, source_target_pairs={{64,0},{128,64},{192,128},{256,192},{320,256},{384,320},{448,384},... | collective-permute-start | bytes 294920 | tf_op jit(solution)/shard_map/ppermute | solution.py:17

commit v4 on v1

--- a/solution.py
+++ b/solution.py
@@ -58,13 +58,12 @@
     dy_move.wait()
 
 
-def turn_kernel(conv_one, conv_two, one, two):
-    width = conv_one.shape[-1]
-    for src, dst in ((conv_two, two), (conv_one, one)):
-        for a in range(3):
-            for b in range(3):
-                for e in range(3):
-                    dst[a, b, :, e * width : (e + 1) * width] = src[2 - a, 2 - b, 2 - e]
+def turn_kernel(src, dst):
+    width = src.shape[-1]
+    for a in range(3):
+        for b in range(3):
+            for e in range(3):
+                dst[a, b, :, e * width : (e + 1) * width] = src[2 - a, 2 - b, 2 - e]
 
 
 def lefts(field, columns, width):
@@ -274,10 +273,11 @@
     held = lax.all_to_all(blocks, ("chip", "core"), 0, 0)
     held = held.reshape(tiles // 8, 8, frames, wide).transpose(2, 1, 0, 3).reshape(frames, tiles, wide)
     turned = array((3, 3, width, 3 * width), BF16)
-    turned_one, turned_two = call(turn_kernel, "vv", (turned, turned), [], 10**9, conv_one, conv_two)
-    held, turned_one, turned_two = lax.optimization_barrier((held, turned_one, turned_two))
+    turned_two = call(turn_kernel, "v", turned, [], 10**9, conv_two)
+    held, turned_two = lax.optimization_barrier((held, turned_two))
     arrived = spread(held)
     own = lax.all_gather(held, "core")
+    turned_one = call(turn_kernel, "v", turned, [], 10**9, conv_one)
     sums = (frames, 4, tiles, width)
     hid = pltpu.VMEM((frames, tiles, 6 * width), BF16)
     z_part, d_part = call(

time: 62.4 us -> 62.4 us (level)
  local copies, waits for them, and re-layouts: 8.07 us -> 3.35 us
  waiting for transfers between devices: 16.4 us -> 21.1 us
    unnamed x20 -> x12, local copies, waits for them, and re-layouts: 7.85 us -> 3.13 us
    all_to_all x1, waiting for transfers between devices: 10.4 us -> 13.8 us  [body(): held = lax.all_to_all(blocks, ('chip', 'core'), 0, 0)]
    ppermute x1, waiting for transfers between devices: 0.04 us -> 1.36 us  [spread(): return lax.ppermute(value, ('tm', 'core'), later + earlier)]
    pallas_call x6 -> x7, Pallas kernels: 10.1 us -> 10 us  [call(): pl.pallas_call(kernel, out_shape=outs, in_specs=[pl.BlockSpec(memory_spac...]
  transfers between devices with their start and end apart: 3 -> 3, of which waited for: 2 -> 3; matrix products, arithmetic and copies ran while one was open for 0% -> 0% of each run, Pallas kernels for 7% -> 7%
where the time goes in v4:
time: 62.4 us; the launch traced here: 62.2 us
  starting transfers between devices  21.9 us (35%)
  waiting for transfers between devices  21.1 us (34%)
  Pallas kernels  10 us (16%)
  blocking collectives  5.61 us (9%)
  local copies, waits for them, and re-layouts  3.35 us (5%)
    all_to_all x1, starting transfers between devices, body(): held = lax.all_to_all(blocks, ('chip', 'core'), 0, 0)  16.6 us
    all_to_all x1, waiting for transfers between devices, body(): held = lax.all_to_all(blocks, ('chip', 'core'), 0, 0)  13.8 us
    pallas_call x7, Pallas kernels, call(): pl.pallas_call(kernel, out_shape=outs, in_specs=[pl.BlockSpec(memory_spac...  10 us
    ppermute x1, waiting for transfers between devices, shifted(): lax.ppermute(value, axis, [(source, source + steps) for source in range(f...  5.95 us
    ppermute x1, starting transfers between devices, spread(): return lax.ppermute(value, ('tm', 'core'), later + earlier)  3.43 us
    all_gather x1, blocking collectives, body(): other = lax.all_gather(arrived, 'core')  3.25 us
    unnamed x12, local copies, waits for them, and re-layouts  3.13 us
    all_gather x1, blocking collectives, body(): own = lax.all_gather(held, 'core')  2.37 us
  transfers between devices with their start and end apart: 3, of which 3 were waited for; matrix products, arithmetic and copies ran while one was open for 0% of the time, Pallas kernels for 7%

profile of v4, /device:TPU:6, one launch (start us, length us, event | category | flops | bytes accessed | tf_op | source)
XLA Modules:
  0.0 62.2 jit_solution(13681893408247214498)
XLA Ops:
  0.0 1.7 %shard_map.73 = bf16[32,2,2,1536]{3,2,1,0:T(2,128)(2,1)} custom-call(s32[2]{0:T(128)} %weight.1, bf16[2,24576]{1,0:T(2,128)(2,1)} %bitcast.24, bf16[2,24576]{1,0:T(2,128)(2,1)} %bitcast.25), custom_call_target="tpu_custom_call" | custom-call | flops 1000000 | bytes 4194304 | tf_op jit(solution)/shard_map/pallas_call | solution.py:247
  1.7 16.6 %all-to-all-start = ((bf16[64,2,1536]{2,1,0:T(2,128)(2,1)}), bf16[64,2,1536]{2,1,0:T(2,128)(2,1)S(1)}, u32[]{:S(2)}, u32[]{:S(2)}) async-start(bf16[64,2,1536]{2,1,0:T(2,128)(2,1)} %bitcast.23), calls=%async_computation | async-start | bytes 786432 | tf_op jit(solution)/shard_map/all_to_all | solution.py:273
  18.3 0.0 copy-start.3
  18.3 1.7 %copy-done.3 = bf16[3,3,3,192,192]{4,3,2,1,0:T(8,128)(2,1)S(1)} copy-done((bf16[3,3,3,192,192]{4,3,2,1,0:T(8,128)(2,1)S(1)}, bf16[3,3,3,192,192]{4,3,2,1,0:T(8,128)(2,1)}, u32[]{:S(2)}) %copy-start.3) | copy-done | bytes 1990680
  20.1 0.0 copy-start
  20.1 0.3 shard_map.74.turned.two
  20.4 0.0 copy-start.1
  20.4 1.4 %copy-done.1 = bf16[3,3,192,576]{3,2,1,0:T(8,128)(2,1)} copy-done((bf16[3,3,192,576]{3,2,1,0:T(8,128)(2,1)}, bf16[3,3,192,576]{3,2,1,0:T(8,128)(2,1)S(1)}, u32[]{:S(2)}) %copy-start.1) | copy-done | bytes 1990680
  21.8 13.8 %all-to-all-done = bf16[64,2,1536]{2,1,0:T(2,128)(2,1)S(1)} async-done(((bf16[64,2,1536]{2,1,0:T(2,128)(2,1)}), bf16[64,2,1536]{2,1,0:T(2,128)(2,1)S(1)}, u32[]{:S(2)}, u32[]{:S(2)}) %all-to-all-start) | async-done | bytes 393248 | tf_op jit(solution)/shard_map/all_to_all | solution.py:273
  35.5 0.2 copy.11
  35.8 0.0 copy-start.2
  35.8 0.0 copy-start.4
  35.8 3.4 %collective-permute-start = (bf16[2,64,1536]{2,1,0:T(8,128)(2,1)S(1)}, bf16[2,64,1536]{2,1,0:T(8,128)(2,1)S(1)}, u32[]{:S(2)}, u32[]{:S(2)}) collective-permute-start(bf16[2,64,1536]{2,1,0:T(8,128)(2,1)S(1)} %bitcast.21), channel_id=1, source_target_pairs={{0,64},{64,128},{128,192},{192,256},{256,320},{320,384},{384,448},... | collective-permute-start | bytes 1179656 | tf_op jit(solution)/shard_map/ppermute | solution.py:24
  39.2 0.0 copy-done
  39.2 0.3 shard_map.76.one
  39.5 2.4 %all-gather.1 = bf16[4,64,1536]{2,1,0:T(8,128)(2,1)S(1)} all-gather(bf16[2,64,1536]{2,1,0:T(8,128)(2,1)S(1)} %bitcast.22), channel_id=3, replica_groups=mesh['tm'=8,'chip'=32,'core'=2] {'core'}, dimensions={0}, use_global_device_ids=true | all-gather | bytes 1179648 | tf_op jit(solution)/shard_map/all_gather | solution.py:279
  41.9 0.0 copy-done.2
  41.9 0.0 copy-done.4
  41.9 0.0 copy-start.5
  41.9 2.3 %shard_map.75 = (f32[2,4,64,192]{3,2,1,0:T(8,128)S(1)}, f32[2,4,64,192]{3,2,1,0:T(8,128)S(1)}) custom-call(bf16[2,2,64,1536]{3,2,1,0:T(8,128)(2,1)S(1)} %bitcast.13, f32[1,192]{1,0:T(1,128)S(1)} %bitcast.16, bf16[3,3,3,192,192]{4,3,2,1,0:T(8,128)(2,1)S(1)} %copy-done, bf16[3,3,192,576]{3,2,1,0:T(8,128)(2,1)S(1)} %copy-done.2), custom_call_target="tpu_custom_call" | custom-call | flops 1019215872 | bytes 4194304 | tf_op jit(solution)/shard_map/pallas_call | solution.py:247
  44.2 1.4 %collective-permute-done = bf16[2,64,1536]{2,1,0:T(8,128)(2,1)S(1)} collective-permute-done((bf16[2,64,1536]{2,1,0:T(8,128)(2,1)S(1)}, bf16[2,64,1536]{2,1,0:T(8,128)(2,1)S(1)}, u32[]{:S(2)}, u32[]{:S(2)}) %collective-permute-start) | collective-permute-done | bytes 393248 | tf_op jit(solution)/shard_map/ppermute | solution.py:24
  45.6 3.2 %all-gather = bf16[4,64,1536]{2,1,0:T(8,128)(2,1)S(1)} all-gather(bf16[2,64,1536]{2,1,0:T(8,128)(2,1)S(1)} %collective-permute-done), channel_id=2, replica_groups=mesh['tm'=8,'chip'=32,'core'=2] {'core'}, dimensions={0}, use_global_device_ids=true | all-gather | bytes 1179648 | tf_op jit(solution)/shard_map/all_gather | solution.py:287
  48.8 0.0 copy-done.5
  48.8 3.4 %shard_map.77 = (bf16[2,64,768]{2,1,0:T(8,128)(2,1)S(1)}, bf16[2,64,384]{2,1,0:T(8,128)(2,1)S(1)}) custom-call(bf16[2,2,64,1536]{3,2,1,0:T(8,128)(2,1)S(1)} %bitcast.15, f32[2,4,64,192]{3,2,1,0:T(8,128)S(1)} %get-tuple-element.17.z_part, f32[2,4,64,192]{3,2,1,0:T(8,128)S(1)} %get-tuple-element.18.d_part, bf16[3,3,192,576]{3,2,1,0:T(8,128)(2,1)S(1)} %copy-done.2, ...), custom_call_target="tpu_custom_call" | custom-call | flops 1019215872 | bytes 4194304 | tf_op jit(solution)/shard_map/pallas_call | solution.py:247
  52.3 1.9 %collective-permute-start.1 = (bf16[2,64,384]{2,1,0:T(8,128)(2,1)S(1)}, bf16[2,64,384]{2,1,0:T(8,128)(2,1)S(1)}, u32[]{:S(2)}, u32[]{:S(2)}) collective-permute-start(bf16[2,64,384]{2,1,0:T(8,128)(2,1)S(1)} %get-tuple-element.19), channel_id=1, source_target_pairs={{64,0},{128,64},{192,128},{256,192},{320,256},{384,320},{448,384},... | collective-permute-start | bytes 294920 | tf_op jit(solution)/shard_map/ppermute | solution.py:17
  54.2 1.2 %shard_map.78 = (f32[2,64,384]{2,1,0:T(8,128)S(1)}, f32[2,64,384]{2,1,0:T(8,128)S(1)}, f32[2,64,384]{2,1,0:T(8,128)S(1)}, f32[2,64,384]{2,1,0:T(8,128)S(1)}) custom-call(bf16[2,2,64,1536]{3,2,1,0:T(8,128)(2,1)S(1)} %bitcast.14, bf16[2,64,768]{2,1,0:T(8,128)(2,1)S(1)} %get-tuple-element.20.d_own, bf16[3,3,192,576]{3,2,1,0:T(8,128)(2,1)S(1)} %shard_map.76.one, ...), custom_call_target="tpu_custom_call" | custom-call | flops 254803968 | bytes 4194304 | tf_op jit(solution)/shard_map/pallas_call | solution.py:247
  55.4 5.9 %collective-permute-done.1.late = bf16[2,64,384]{2,1,0:T(8,128)(2,1)S(1)} collective-permute-done((bf16[2,64,384]{2,1,0:T(8,128)(2,1)S(1)}, bf16[2,64,384]{2,1,0:T(8,128)(2,1)S(1)}, u32[]{:S(2)}, u32[]{:S(2)}) %collective-permute-start.1) | collective-permute-done | bytes 98336 | tf_op jit(solution)/shard_map/ppermute | solution.py:17
  61.4 0.8 %shard_map.79 = bf16[2,64,384]{2,1,0:T(8,128)(2,1)} custom-call(bf16[2,64,384]{2,1,0:T(8,128)(2,1)S(1)} %collective-permute-done.1.late, f32[2,64,384]{2,1,0:T(8,128)S(1)} %get-tuple-element.21.base, f32[2,64,384]{2,1,0:T(8,128)S(1)} %get-tuple-element.22.slope, f32[2,64,384]{2,1,0:T(8,128)S(1)} %get-tuple-element.23.along, ...), custom_call_target="tpu_custom_call" | custom-call | flops 42467328 | bytes 4194304 | tf_op jit(solution)/shard_map/pallas_call | solution.py:247
Async XLA Ops:
  1.7 33.8 %all-to-all-start = ((bf16[64,2,1536]{2,1,0:T(2,128)(2,1)}), bf16[64,2,1536]{2,1,0:T(2,128)(2,1)S(1)}, u32[]{:S(2)}, u32[]{:S(2)}) async-start(bf16[64,2,1536]{2,1,0:T(2,128)(2,1)} %bitcast.23), calls=%async_computation | async-start | bytes 786432 | tf_op jit(solution)/shard_map/all_to_all | solution.py:273
  18.3 1.8 %copy-start.3 = (bf16[3,3,3,192,192]{4,3,2,1,0:T(8,128)(2,1)S(1)}, bf16[3,3,3,192,192]{4,3,2,1,0:T(8,128)(2,1)}, u32[]{:S(2)}) copy-start(bf16[3,3,3,192,192]{4,3,2,1,0:T(8,128)(2,1)} %src.2) | copy-start | bytes 5971972
  20.1 19.1 %copy-start = (bf16[3,3,3,192,192]{4,3,2,1,0:T(8,128)(2,1)S(1)}, bf16[3,3,3,192,192]{4,3,2,1,0:T(8,128)(2,1)}, u32[]{:S(2)}) copy-start(bf16[3,3,3,192,192]{4,3,2,1,0:T(8,128)(2,1)} %conv_one.3) | copy-start | bytes 5971972
  20.4 1.4 %copy-start.1 = (bf16[3,3,192,576]{3,2,1,0:T(8,128)(2,1)}, bf16[3,3,192,576]{3,2,1,0:T(8,128)(2,1)S(1)}, u32[]{:S(2)}) copy-start(bf16[3,3,192,576]{3,2,1,0:T(8,128)(2,1)S(1)} %shard_map.74.turned.two) | copy-start | bytes 5971972
  35.8 6.1 %copy-start.2 = (bf16[3,3,192,576]{3,2,1,0:T(8,128)(2,1)S(1)}, bf16[3,3,192,576]{3,2,1,0:T(8,128)(2,1)}, u32[]{:S(2)}) copy-start(bf16[3,3,192,576]{3,2,1,0:T(8,128)(2,1)} %copy-done.1) | copy-start | bytes 5971972
  35.8 6.1 %copy-start.4 = (f32[192]{0:T(256)S(1)}, f32[192]{0:T(256)}, u32[]{:S(2)}) copy-start(f32[192]{0:T(256)} %param.10) | copy-start | bytes 2308
  35.8 9.8 %collective-permute-start = (bf16[2,64,1536]{2,1,0:T(8,128)(2,1)S(1)}, bf16[2,64,1536]{2,1,0:T(8,128)(2,1)S(1)}, u32[]{:S(2)}, u32[]{:S(2)}) collective-permute-start(bf16[2,64,1536]{2,1,0:T(8,128)(2,1)S(1)} %bitcast.21), channel_id=1, source_target_pairs={{0,64},{64,128},{128,192},{192,256},{256,320},{320,384},{384,448},... | collective-permute-start | bytes 1179656 | tf_op jit(solution)/shard_map/ppermute | solution.py:24
  41.9 6.9 %copy-start.5 = (f32[192]{0:T(256)S(1)}, f32[192]{0:T(256)}, u32[]{:S(2)}) copy-start(f32[192]{0:T(256)} %param.12) | copy-start | bytes 2308
  52.3 9.1 %collective-permute-start.1 = (bf16[2,64,384]{2,1,0:T(8,128)(2,1)S(1)}, bf16[2,64,384]{2,1,0:T(8,128)(2,1)S(1)}, u32[]{:S(2)}, u32[]{:S(2)}) collective-permute-start(bf16[2,64,384]{2,1,0:T(8,128)(2,1)S(1)} %get-tuple-element.19), channel_id=1, source_target_pairs={{64,0},{128,64},{192,128},{256,192},{320,256},{384,320},{448,384},... | collective-permute-start | bytes 294920 | tf_op jit(solution)/shard_map/ppermute | solution.py:17
